TPU v7x, 512 devices: a whole 4x8x8 slice. The times are simulated.
512 devices in a mesh: res: 128 (over z, y, core), dp: 4 (over x).
Axes of the slice: x: 4, y: 8, z: 8, core: 2. Of those that a mesh axis runs over, the one named last changes fastest.
Arguments:
- aligned_chain_features: bfloat16 [512, 256, 256], P('dp', 'res'), parts along dimension 0, may hold values from -6 to 6
- pair_representation_state: bfloat16 [1024, 256, 128], P(('dp', 'res')), parts along dimension 0, may hold values from -6 to 6
- gap_block_flags: int32 [512, 2], P('dp'), parts along dimension 0, may hold values from 0 to 1, as said below
- pair_norm_gain: float32 [128], replicated, may hold values from 0.1 to 1.9
- pair_head_weight: bfloat16 [128, 8], replicated, may hold values from -0.5 to 0.5
- horizontal_scaling_factor: float32 [256], replicated, may hold values from 0.1 to 1.9
- row_input_weight: bfloat16 [256, 1024], replicated, may hold values from -2 to 2
- horizontal_final_matrix: bfloat16 [256, 256], replicated, may hold values from -0.375 to 0.375
- vertical_scaling_factor: float32 [256], replicated, may hold values from 0.1 to 1.9
- column_input_weight: bfloat16 [256, 1024], replicated, may hold values from -2 to 2
- vertical_final_matrix: bfloat16 [256, 256], replicated, may hold values from -0.375 to 0.375
- feedforward_scaling_factor: float32 [256], replicated, may hold values from 0.1 to 1.9
- feedforward_widen_matrix: bfloat16 [256, 1024], replicated, may hold values from -0.375 to 0.375
- feedforward_shrink_matrix: bfloat16 [1024, 256], replicated, may hold values from -0.1875 to 0.1875
Outputs:
- msa_out: bfloat16 [512, 256, 256], P('dp', 'res'), parts along dimension 0
There are 4 independent parts, one for each index of `dp`. A program takes and returns all parts, laid end to end along the dimension named above; an argument that names none is the same for every part. Nothing has to cross between parts.
Inputs may be any that keep to these rules, and one draw needn't show every extreme that they name: `gap_block_flags`: row 0 holds no gap block, and every row has at least one block that is not a gap.
All inputs are finite; a program needn't handle non-finite values.
Results may differ from a plain program's by a relative error of at most 0.015.
The roundings to bfloat16 on the way count: a program that leaves them out, or rounds other values in their place, can miss the bound.
Values may be sent and summed in bfloat16 or wider, within the bound.
A program may use at most 64 MiB of HBM per device.

v0:
```python
import jax
import jax.numpy as jnp
from jax import lax
from jax.sharding import PartitionSpec as P

BLOCK = 128


EPSILON = 1e-05
MASKED_SCORE = -1000000000.0


def layer_normalize(inputs, scale_gain):
    values_f = inputs.astype(jnp.float32)
    centred = values_f - jnp.mean(values_f, axis=-1, keepdims=True)
    spread = jnp.mean(centred * centred, axis=-1, keepdims=True)
    return centred * lax.rsqrt(spread + EPSILON) * scale_gain


def project(normed_bf, weights_in, head_count, head_depth):
    projected = jnp.dot(normed_bf, weights_in, preferred_element_type=jnp.float32)
    projected = projected.reshape(projected.shape[:-1] + (4, head_count, head_depth))
    queries = (projected[..., 0, :, :] * head_depth ** (-0.5)).astype(jnp.bfloat16)
    keys_bf = projected[..., 1, :, :].astype(jnp.bfloat16)
    values_bf = projected[..., 2, :, :].astype(jnp.bfloat16)
    gates = jax.nn.sigmoid(projected[..., 3, :, :])
    return (queries, keys_bf, values_bf, gates)


def attend_dense(queries, keys_bf, values_bf, bias_piece, masked):
    scores = jnp.einsum("qhd,khd->hqk", queries, keys_bf, preferred_element_type=jnp.float32)
    scores = scores + bias_piece.astype(jnp.float32)
    scores = jnp.where(masked[None, None, :], MASKED_SCORE, scores)
    weights_bf = jax.nn.softmax(scores, axis=-1).astype(jnp.bfloat16)
    return jnp.einsum("hqk,khd->qhd", weights_bf, values_bf, preferred_element_type=jnp.float32)


def body(
    aligned_chain_features,
    pair_representation_state,
    gap_block_flags,
    pair_norm_gain,
    pair_head_weight,
    horizontal_scaling_factor,
    row_input_weight,
    horizontal_final_matrix,
    vertical_scaling_factor,
    column_input_weight,
    vertical_final_matrix,
    feedforward_scaling_factor,
    feedforward_widen_matrix,
    feedforward_shrink_matrix,
):
    head_count = pair_head_weight.shape[1]
    head_depth = horizontal_final_matrix.shape[0] // head_count
    pair_normed = layer_normalize(pair_representation_state, pair_norm_gain).astype(jnp.bfloat16)
    bias_local = jnp.einsum(
        "ijc,ch->hij", pair_normed, pair_head_weight, preferred_element_type=jnp.float32
    ).astype(jnp.bfloat16)
    sequence_rows = lax.all_to_all(
        aligned_chain_features, "res", split_axis=0, concat_axis=1, tiled=True
    )
    local_seqs, residues = (sequence_rows.shape[0], sequence_rows.shape[1])
    gap_local = lax.dynamic_slice_in_dim(
        gap_block_flags, lax.axis_index("res") * local_seqs, local_seqs, 0
    )
    row_normed = layer_normalize(sequence_rows, horizontal_scaling_factor).astype(jnp.bfloat16)
    queries, keys_all, values_all, gates_all = project(
        row_normed, row_input_weight, head_count, head_depth
    )
    bias_all = lax.all_gather(bias_local, "res", axis=1, tiled=True)
    row_count = bias_all.shape[1]

    def per_sequence(sequence_entries):
        (
            sequence_queries,
            sequence_keys,
            sequence_values,
            sequence_gates,
            sequence_alignment,
            sequence_gap_row,
        ) = sequence_entries
        attended = attend_dense(
            sequence_queries,
            sequence_keys,
            sequence_values,
            bias_all,
            jnp.repeat(sequence_gap_row, BLOCK) == 1,
        )
        gated_out = (
            (attended * sequence_gates)
            .astype(jnp.bfloat16)
            .reshape(row_count, head_count * head_depth)
        )
        layer_update = jnp.dot(
            gated_out, horizontal_final_matrix, preferred_element_type=jnp.float32
        )
        return (sequence_alignment.astype(jnp.float32) + layer_update).astype(jnp.bfloat16)

    blocks_out = lax.map(
        per_sequence, (queries, keys_all, values_all, gates_all, sequence_rows, gap_local)
    )
    res_rows = lax.all_to_all(blocks_out, "res", split_axis=1, concat_axis=0, tiled=True)
    col_normed = layer_normalize(res_rows, vertical_scaling_factor).astype(jnp.bfloat16)
    col_q, col_k, col_v, col_gates = project(
        col_normed, column_input_weight, head_count, head_depth
    )
    total_seqs, local_res = (res_rows.shape[0], res_rows.shape[1])
    block_total = gap_block_flags.shape[1]
    global_res = lax.axis_index("res") * local_res + jnp.arange(local_res, dtype=jnp.int32)
    one_hot = (
        global_res[:, None] // BLOCK == jnp.arange(block_total, dtype=jnp.int32)[None, :]
    ).astype(jnp.int32)
    col_gaps = jnp.sum(gap_block_flags[:, None, :] * one_hot[None, :, :], axis=2)
    col_scores = jnp.einsum("srhd,trhd->rhst", col_q, col_k, preferred_element_type=jnp.float32)
    col_scores = jnp.where(
        (jnp.transpose(col_gaps) == 1)[:, None, None, :], MASKED_SCORE, col_scores
    )
    col_weights = jax.nn.softmax(col_scores, axis=-1).astype(jnp.bfloat16)
    col_attended = jnp.einsum(
        "rhst,trhd->srhd", col_weights, col_v, preferred_element_type=jnp.float32
    )
    col_gated = (
        (col_attended * col_gates)
        .astype(jnp.bfloat16)
        .reshape(total_seqs, local_res, head_count * head_depth)
    )
    alignment_second = (
        res_rows.astype(jnp.float32)
        + jnp.dot(col_gated, vertical_final_matrix, preferred_element_type=jnp.float32)
    ).astype(jnp.bfloat16)
    transition_normed = layer_normalize(alignment_second, feedforward_scaling_factor).astype(
        jnp.bfloat16
    )
    tr_hidden = jax.nn.relu(
        jnp.dot(transition_normed, feedforward_widen_matrix, preferred_element_type=jnp.float32)
    ).astype(jnp.bfloat16)
    return (
        alignment_second.astype(jnp.float32)
        + jnp.dot(tr_hidden, feedforward_shrink_matrix, preferred_element_type=jnp.float32)
    ).astype(jnp.bfloat16)


def solution(mesh):
    placed = (
        P("dp", "res", None),
        P(("dp", "res"), None, None),
        P("dp", None),
        P(),
        P(),
        P(),
        P(),
        P(),
        P(),
        P(),
        P(),
        P(),
        P(),
        P(),
    )
    return jax.shard_map(
        body, mesh=mesh, in_specs=placed, out_specs=P("dp", "res", None), check_vma=False
    )
```

profile of v0, /device:TPU:1, one launch (start us, length us, event | category | flops | bytes accessed | tf_op | source)
XLA Modules:
  0.0 144.8 jit_solution(7586476463166801877)
XLA Ops:
  6.5 0.0 copy-start
  6.5 0.0 copy-start.2
  6.5 0.0 all-gather.2.cloned.1.call-start
  6.5 1.1 convert_reduce_fusion
  7.7 1.2 fusion.23
  8.8 1.8 %fusion.16 = bf16[8,2,256]{2,0,1:T(8,128)(2,1)} fusion(bf16[2,256,128]{2,1,0:T(8,128)(2,1)} %param.15, f32[128]{0:T(128)} %param.17, f32[2,256]{1,0:T(2,128)S(1)} %add_rsqrt_fusion, f32[2,256]{1,0:T(2,128)S(1)} %broadcast_multiply_fusion.1, bf16[128,8]{0,1:T(8,128)(2,1)} %param.18), kind=kOutput, calls=%fused_computation.27 | convolution fusion | flops 1380352 | bytes 145920 | tf_op jit(solution)/shard_map/ijc,ch->hij/dot_general | solution.py:57
  10.7 0.0 all-gather.2.cloned.1.call-update
  10.7 18.4 %all-to-all-start = ((bf16[128,2,256]{2,1,0:T(2,128)(2,1)}), bf16[128,2,256]{2,1,0:T(2,128)(2,1)S(1)}, u32[]{:S(2)}, u32[]{:S(2)}) async-start(bf16[128,2,256]{2,1,0:T(2,128)(2,1)} %param.14), calls=%async_computation | async-start | bytes 262144 | tf_op jit(solution)/shard_map/all_to_all | solution.py:60
  29.1 0.9 compare_reduce_fusion
  30.0 0.1 broadcast_bitcast_fusion
  30.1 0.0 copy-done.2
  30.1 0.0 copy-start.7
  30.1 0.2 copy.93
  30.3 0.1 compare_convert_fusion
  30.4 11.5 %all-to-all-done = bf16[128,2,256]{2,1,0:T(2,128)(2,1)S(1)} async-done(((bf16[128,2,256]{2,1,0:T(2,128)(2,1)}), bf16[128,2,256]{2,1,0:T(2,128)(2,1)S(1)}, u32[]{:S(2)}, u32[]{:S(2)}) %all-to-all-start) | async-done | bytes 131104 | tf_op jit(solution)/shard_map/all_to_all | solution.py:60
  41.9 0.2 convert_reduce_fusion.4
  42.1 0.1 div.74
  42.3 0.2 multiply_reduce_fusion.2
  42.5 0.1 rsqrt.38
  42.6 0.0 copy-done.7
  42.6 0.3 multiply_convert_fusion.1
  43.0 0.1 reshape.330
  43.1 1.1 fusion.86
  44.2 0.0 copy-start.1
  44.2 51.8 %all-gather.2.cloned.1.call-done = bf16[8,256,256]{2,0,1:T(8,128)(2,1)} async-done(((bf16[8,2,256]{2,0,1:T(8,128)(2,1)}), bf16[8,256,256]{2,0,1:T(8,128)(2,1)}) %all-gather.2.cloned.1.call-update) | async-done | bytes 1048592 | tf_op jit(solution)/shard_map/all_gather | solution.py:71
  96.0 1.6 %copy.94 = bf16[8,256,256]{1,2,0:T(8,128)(2,1)S(1)} copy(bf16[8,256,256]{2,0,1:T(8,128)(2,1)} %all-gather.2.cloned.1.call-done) | data formatting | bytes 2097152 | tf_op jit(solution)/shard_map/all_gather | solution.py:71
  97.6 0.0 copy-done.1
  97.7 0.9 fusion.87
  98.5 0.0 copy-start.4
  98.6 1.8 %fusion.14 = bf16[256,8,32]{0,2,1:T(8,128)(2,1)} fusion(f32[8,256]{1,0:T(8,128)S(1)} %fusion.87, f32[1,256,4,8,32]{1,4,3,2,0:T(8,128)S(1)} %get-tuple-element.26, bf16[1,256,4,8,32]{1,4,3,2,0:T(8,128)(2,1)S(1)} %copy-done.1, bf16[8,256,256]{1,2,0:T(8,128)(2,1)S(1)} %copy.94, pred[256]{0:T(512)(128)(4,1)S(1)} %broadcast_bitcast_fusion), kind=kOutput, calls=%fused_computation.24 | convolution fusion | flops 70715648 | bytes 1974784 | tf_op jit(solution)/shard_map/while/body/eval_jaxpr/hqk,khd->qhd/dot_general | solution.py:35
  100.3 0.0 copy-start.6
  100.3 0.0 copy-done.4
  100.3 1.2 fusion.15
  101.5 0.2 copy.119
  101.7 0.5 broadcast.286
  102.2 1.4 reduce.10
  103.7 0.7 reshape.341
  104.4 8.2 %all-to-all-start.1 = ((bf16[128,2,256]{2,1,0:T(2,128)(2,1)}), bf16[128,2,256]{2,1,0:T(2,128)(2,1)S(1)}, u32[]{:S(2)}, u32[]{:S(2)}) async-start(bf16[128,2,256]{2,1,0:T(2,128)(2,1)} %reshape.341), calls=%async_computation.1 | async-start | bytes 262144 | tf_op jit(solution)/shard_map/all_to_all | solution.py:103
  112.6 0.0 copy-done.6
  112.6 0.1 multiply_reduce_fusion.3
  112.7 0.0 copy-done.3
  112.7 0.0 copy-start.8
  112.7 0.2 copy.97
  112.9 12.4 %all-to-all-done.1 = bf16[128,2,256]{2,1,0:T(2,128)(2,1)S(1)} async-done(((bf16[128,2,256]{2,1,0:T(2,128)(2,1)}), bf16[128,2,256]{2,1,0:T(2,128)(2,1)S(1)}, u32[]{:S(2)}, u32[]{:S(2)}) %all-to-all-start.1) | async-done | bytes 131104 | tf_op jit(solution)/shard_map/all_to_all | solution.py:103
  125.3 0.1 reshape.342
  125.4 1.3 convert_reduce_fusion.2
  126.8 3.6 %multiply_reduce_fusion.1 = f32[256]{0:T(256)S(1)} fusion(f32[256]{0:T(256)S(1)} %broadcast_multiply_fusion.2, bf16[256,1,256]{2,1,0:T(2,128)(2,1)S(1)} %reshape.342), kind=kLoop, calls=%fused_computation.59 | loop fusion | flops 261888 | bytes 133120 | tf_op jit(solution)/shard_map/reduce_sum | solution.py:16
  130.4 0.0 copy-done.8
  130.4 1.6 %convert_reduce_fusion.3 = bf16[256,256]{1,0:T(8,128)(2,1)S(1)} fusion(f32[256]{0:T(256)S(1)} %add_rsqrt_fusion.2, f32[256]{0:T(256)S(1)} %broadcast_multiply_fusion.2, f32[256]{0:T(256)S(1)} %copy-done.8, bf16[256,1,256]{2,1,0:T(2,128)(2,1)S(1)} %reshape.342), kind=kLoop, calls=%fused_computation.58 | loop fusion | flops 327680 | bytes 265216 | tf_op jit(solution)/shard_map/convert_element_type | solution.py:104
  131.9 0.1 convert_element_type.184
  132.0 0.1 reshape.329
  132.1 0.3 fusion.90
  132.5 1.5 %fusion.91 = (f32[2,8,128]{2,1,0:T(8,128)S(1)}, f32[2,8,128,128]{2,3,1,0:T(8,128)}) fusion(pred[2,128]{1,0:T(4,128)(4,1)S(1)} %compare_bitcast_fusion, f32[128,2,4,8,32]{0,4,3,2,1:T(8,128)S(1)} %get-tuple-element.28, bf16[128,2,4,8,32]{0,4,3,2,1:T(8,128)(2,1)S(1)} %get-tuple-element.27), kind=kOutput, calls=%fused_computation.114 | convolution fusion | flops 17694848 | bytes 1450496 | tf_op jit(solution)/shard_map/sub | solution.py:119
  134.0 0.0 copy-start.5
  134.0 1.5 %fusion.10 = bf16[128,2,8,32]{0,3,2,1:T(8,128)(2,1)S(1)} fusion(f32[2,8,128,128]{2,3,1,0:T(8,128)} %get-tuple-element.40, f32[2,8,128]{2,1,0:T(8,128)S(1)} %get-tuple-element.29, f32[128,2,4,8,32]{0,4,3,2,1:T(8,128)S(1)} %get-tuple-element.28, bf16[128,2,4,8,32]{0,4,3,2,1:T(8,128)(2,1)S(1)} %get-tuple-element.27), kind=kOutput, calls=%fused_computation.20 | convolution fusion | flops 17629184 | bytes 1581056 | tf_op jit(solution)/shard_map/rhst,trhd->srhd/dot_general | solution.py:120
  135.5 0.0 copy-start.10
  135.5 0.0 copy-done.5
  135.5 0.3 fusion.94
  135.8 0.2 multiply_reduce_fusion
  136.0 0.0 copy-done
  136.0 0.5 copy-done.9
  136.5 0.0 copy-done.10
  136.5 0.6 fusion.13
  137.1 0.8 copy.102
  (14 shorter events, 0.2 us)
Async XLA Ops:
  6.5 129.5 %copy-start = (bf16[1024,256]{1,0:T(8,128)(2,1)S(1)}, bf16[1024,256]{1,0:T(8,128)(2,1)}, u32[]{:S(2)}) copy-start(bf16[1024,256]{1,0:T(8,128)(2,1)} %param.27) | copy-start | bytes 1572868
  6.5 23.6 %copy-start.2 = (bf16[256,1024]{1,0:T(8,128)(2,1)S(1)}, bf16[256,1024]{1,0:T(8,128)(2,1)}, u32[]{:S(2)}) copy-start(bf16[256,1024]{1,0:T(8,128)(2,1)} %param.20) | copy-start | bytes 1572868
  6.5 89.5 %all-gather.2.cloned.1.call-start = ((), (), s32[]{:S(2)}) async-start(), calls=%async_computation.2 | async-start | bytes 1056768 | tf_op jit(solution)/shard_map/all_gather | solution.py:71
  10.7 31.2 %all-to-all-start = ((bf16[128,2,256]{2,1,0:T(2,128)(2,1)}), bf16[128,2,256]{2,1,0:T(2,128)(2,1)S(1)}, u32[]{:S(2)}, u32[]{:S(2)}) async-start(bf16[128,2,256]{2,1,0:T(2,128)(2,1)} %param.14), calls=%async_computation | async-start | bytes 262144 | tf_op jit(solution)/shard_map/all_to_all | solution.py:60
  30.1 12.5 %copy-start.7 = (f32[256]{0:T(256)S(1)}, f32[256]{0:T(256)}, u32[]{:S(2)}) copy-start(f32[256]{0:T(256)} %param.19) | copy-start | bytes 3076
  44.2 53.4 %copy-start.1 = (bf16[1,256,4,8,32]{1,4,3,2,0:T(8,128)(2,1)S(1)}, bf16[1,256,4,8,32]{1,4,3,2,0:T(8,128)(2,1)}, u32[]{:S(2)}) copy-start(bf16[1,256,4,8,32]{1,4,3,2,0:T(8,128)(2,1)} %get-tuple-element.25) | copy-start | bytes 1572868
  98.5 1.8 %copy-start.4 = (bf16[256,256]{1,0:T(8,128)(2,1)S(1)}, bf16[256,256]{1,0:T(8,128)(2,1)}, u32[]{:S(2)}) copy-start(bf16[256,256]{1,0:T(8,128)(2,1)} %param.21) | copy-start | bytes 393220
  100.3 12.3 %copy-start.6 = (s32[128,2]{0,1:T(2,128)S(1)}, s32[128,2]{0,1:T(2,128)}, u32[]{:S(2)}) copy-start(s32[128,2]{0,1:T(2,128)} %param.16) | copy-start | bytes 3076
  100.3 12.4 %copy-start.3 = (bf16[256,1024]{1,0:T(8,128)(2,1)S(1)}, bf16[256,1024]{1,0:T(8,128)(2,1)}, u32[]{:S(2)}) copy-start(bf16[256,1024]{1,0:T(8,128)(2,1)} %param.23) | copy-start | bytes 1572868
  104.4 21.0 %all-to-all-start.1 = ((bf16[128,2,256]{2,1,0:T(2,128)(2,1)}), bf16[128,2,256]{2,1,0:T(2,128)(2,1)S(1)}, u32[]{:S(2)}, u32[]{:S(2)}) async-start(bf16[128,2,256]{2,1,0:T(2,128)(2,1)} %reshape.341), calls=%async_computation.1 | async-start | bytes 262144 | tf_op jit(solution)/shard_map/all_to_all | solution.py:103
  112.7 17.6 %copy-start.8 = (f32[256]{0:T(256)S(1)}, f32[256]{0:T(256)}, u32[]{:S(2)}) copy-start(f32[256]{0:T(256)} %param.22) | copy-start | bytes 3076
  134.0 1.5 %copy-start.5 = (bf16[256,256]{1,0:T(8,128)(2,1)S(1)}, bf16[256,256]{1,0:T(8,128)(2,1)}, u32[]{:S(2)}) copy-start(bf16[256,256]{1,0:T(8,128)(2,1)} %param.24) | copy-start | bytes 393220
  135.5 1.0 copy-start.9
  135.5 1.0 copy-start.10
Sparse Core Ops, SparseCore 0:
  10.8 85.1 all-gather.1
where the time goes:
time: 145 us
  waiting for transfers between devices  75.6 us (52%)
  starting transfers between devices  26.7 us (18%)
  between operations  13.7 us (9%)
  other arithmetic  12.1 us (8%)
  matrix products  11.1 us (8%)
  local copies, waits for them, and re-layouts  5.59 us (4%)
    all_gather x1, waiting for transfers between devices, body(): bias_all = lax.all_gather(bias_local, 'res', axis=1, tiled=True)  51.8 us
    all_to_all x1, starting transfers between devices, body(): lax.all_to_all(aligned_chain_features, 'res', split_axis=0, concat_axis=1...  18.4 us
    all_to_all x1, waiting for transfers between devices, body(): lax.all_to_all(blocks_out, 'res', split_axis=1, concat_axis=0, tiled=True)  12.4 us
    all_to_all x1, waiting for transfers between devices, body(): lax.all_to_all(aligned_chain_features, 'res', split_axis=0, concat_axis=1...  11.5 us
    all_to_all x1, starting transfers between devices, body(): lax.all_to_all(blocks_out, 'res', split_axis=1, concat_axis=0, tiled=True)  8.23 us
    reduce_sum x4, other arithmetic, layer_normalize(): spread = jnp.mean(centred * centred, axis=-1, keepdims=True)  5.09 us
  transfers between devices with their start and end apart: 3, of which 3 were waited for; matrix products, arithmetic and copies ran while one was open for 3% of the time, Pallas kernels for 0%

commit v1 on v0

v1 whole, which is shorter than its diff:
```python
import jax
import jax.numpy as jnp
from jax import lax
from jax.experimental import pallas as pl
from jax.experimental.pallas import tpu as pltpu
from jax.sharding import PartitionSpec as P

EPSILON = 1e-05
MASKED_SCORE = -1000000000.0
HEADS = 8
DEPTH = 32
BF = jnp.bfloat16
F32 = jnp.float32
MESH = pl.DeviceIdType.MESH
NT = (((1,), (1,)), ((), ()))


def normalize(values, gain):
    centred = values - jnp.mean(values, axis=-1, keepdims=True)
    spread = jnp.mean(centred * centred, axis=-1, keepdims=True)
    return (centred * lax.rsqrt(spread + EPSILON) * gain).astype(BF)


def mm(a, b):
    return jnp.dot(a, b, preferred_element_type=F32)


def mm_nt(a, b):
    return lax.dot_general(a, b, NT, preferred_element_type=F32)


def selector(source_of, rows):
    o = lax.broadcasted_iota(jnp.int32, (rows, rows), 0)
    i = lax.broadcasted_iota(jnp.int32, (rows, rows), 1)
    return jnp.where(source_of(o) == i, 1.0, 0.0).astype(F32).astype(BF)


def pick(one_hot, rows):
    return mm(one_hot, rows).astype(BF)


def head_lanes(h, rows, width=256):
    lane = lax.broadcasted_iota(jnp.int32, (rows, width), 1)
    return lane // DEPTH == h


def remote(src, dst, send, recv, device):
    return pltpu.make_async_remote_copy(
        src_ref=src,
        dst_ref=dst,
        send_sem=send,
        recv_sem=recv,
        device_id={"res": device},
        device_id_type=MESH,
    )


def row_kernel(
    x_ref, pair_ref, flags_ref, pgain_ref, pw_ref, gain_ref, win_hbm, wout_hbm,
    out_ref,
    win, wout, bloc, xmid, xsend, xrows, bmid, bsend, bias, m1, cmid, csend,
    wsem, xa_s, xa_r, ba_s, ba_r, xb_s, xb_r, bb_s, bb_r, dd_s, dd_r, ca_s, ca_r, cb_s, cb_r,
):
    me = lax.axis_index("res")
    z = me // 16
    k = lax.rem(me, 16)
    y = k // 2
    c = lax.rem(me, 2)
    sib = me + 1 - 2 * c

    load_in = pltpu.make_async_copy(win_hbm, win, wsem.at[0])
    load_out = pltpu.make_async_copy(wout_hbm, wout, wsem.at[1])
    load_in.start()
    load_out.start()

    barrier = pltpu.get_barrier_semaphore()

    def greet(device):
        pl.semaphore_signal(barrier, inc=1, device_id={"res": device}, device_id_type=MESH)

    for j in (4, 3, 5, 2, 6, 1, 7):
        greet(lax.rem(z + j, 8) * 16 + k)
        greet(lax.rem(z + j, 8) * 16 + y * 2 + 1 - c)
    for j in (8, 7, 9, 6, 10, 5, 11, 4, 12, 3, 13, 2, 14, 1, 15):
        greet(z * 16 + lax.rem(k + j, 16))

    normed = normalize(pair_ref[...].astype(F32), pgain_ref[...])
    biases = mm_nt(pw_ref[...], normed).astype(BF)
    bloc[0] = jnp.concatenate([biases[:, 0:128], biases[:, 256:384]], axis=0)
    bloc[1] = jnp.concatenate([biases[:, 128:256], biases[:, 384:512]], axis=0)

    pl.semaphore_wait(barrier, 29)

    for j in (8, 7, 9, 6, 10, 5, 11, 4, 12, 3, 13, 2, 14, 1, 15):
        kp = lax.rem(k + j, 16)
        remote(x_ref.at[kp], xmid.at[k], xa_s, xa_r, z * 16 + kp).start()
    xmid[k] = x_ref[k]
    for j in (4, 3, 5, 2, 6, 1, 7):
        yp = lax.rem(y + j, 8)
        remote(bloc.at[0], bmid.at[k], ba_s, ba_r, z * 16 + yp * 2).start()
        zp = lax.rem(z + j, 8)
        remote(bloc.at[1], bmid.at[z * 2 + c], ba_s, ba_r, zp * 16 + y * 2 + 1).start()

    @pl.when(c == 0)
    def _():
        remote(bloc.at[1], bmid.at[z * 2], ba_s, ba_r, sib).start()
        bmid[k] = bloc[0]

    @pl.when(c == 1)
    def _():
        remote(bloc.at[0], bmid.at[k], ba_s, ba_r, sib).start()
        bmid[z * 2 + 1] = bloc[1]

    by_z = selector(lambda o: lax.rem(o, 32) // 2 * 16 + o // 32 * 2 + lax.rem(o, 2), 256)
    by_h = selector(lambda o: lax.rem(o, 32) // 2 * 16 + lax.rem(o, 2) * 8 + o // 32, 256)
    by_k = selector(lambda o: lax.rem(o, 16) // 2 * 32 + o // 16 * 2 + lax.rem(o, 2), 256)
    natural = selector(lambda o: lax.rem(o, 32) // 4 * 32 + o // 32 * 4 + lax.rem(o, 4), 256)

    remote(xmid.at[pl.ds(0, 15)], xmid.at[pl.ds(0, 15)], xa_s, xa_r, sib).wait_recv()
    xsend[...] = pick(by_z, xmid[...].reshape(256, 256)).reshape(8, 32, 256)
    for j in (4, 3, 5, 2, 6, 1, 7):
        zp = lax.rem(z + j, 8)
        remote(xsend.at[zp], xrows.at[z], xb_s, xb_r, zp * 16 + k).start()
    xrows[z] = xsend[z]

    remote(bmid.at[pl.ds(0, 15)], bmid.at[pl.ds(0, 15)], ba_s, ba_r, sib).wait_recv()
    bsend[...] = pick(by_h, bmid[...].reshape(256, 128)).reshape(8, 32, 128)
    place = pl.multiple_of(jnp.where(c == 0, z, y) * 32, 32)
    for g in range(4):
        for j in (4, 3, 5, 2, 6, 1, 7):
            peer = jnp.where(
                c == 0, lax.rem(z + j, 8) * 16 + k, z * 16 + lax.rem(y + j, 8) * 2 + c
            )
            remote(
                bsend.at[pl.ds(2 * g, 2)],
                bias.at[c, pl.ds(2 * g, 2), pl.ds(place, 32)],
                bb_s.at[g],
                bb_r.at[g],
                peer,
            ).start()
    bias[c, :, pl.ds(place, 32), :] = bsend[...]

    def arrived(g):
        part = bias.at[0, pl.ds(2 * g, 2), pl.ds(0, 224)]
        remote(part, part, bb_s.at[g], bb_r.at[g], sib).wait_recv()
        part = bias.at[c, pl.ds(2 * g, 2)]
        remote(part, part, dd_s.at[g], dd_r.at[g], sib).start()

    def complete(g):
        part = bias.at[c, pl.ds(2 * g, 2)]
        remote(part, part, dd_s.at[g], dd_r.at[g], sib).wait_recv()

    seq = lax.broadcasted_iota(jnp.int32, (2, 128), 1)
    gaps = jnp.sum(jnp.where(seq == 8 * k + z, flags_ref[...], 0), axis=1, keepdims=True)
    half = lax.broadcasted_iota(jnp.int32, (1, 256), 1) // 128
    masked = jnp.where(half == 0, gaps[0:1], gaps[1:2]) == 1

    load_in.wait()
    load_out.wait()
    remote(xrows.at[pl.ds(0, 7)], xrows.at[pl.ds(0, 7)], xb_s, xb_r, sib).wait_recv()
    rows_bf = xrows[...].reshape(256, 256)
    rows = rows_bf.astype(F32)
    row_normed = normalize(rows, gain_ref[...])
    queries = (mm(row_normed, win[:, 0:256]) * DEPTH ** (-0.5)).astype(BF)
    keys = mm(row_normed, win[:, 256:512]).astype(BF)
    values = mm(row_normed, win[:, 512:768]).astype(BF)
    gates = jax.nn.sigmoid(mm(row_normed, win[:, 768:1024]))

    arrived(0)
    arrived(1)
    total = jnp.zeros((256, 512), F32)
    for g in range(4):
        complete(g)
        exps = []
        weights = []
        for h in (2 * g, 2 * g + 1):
            mine = head_lanes(h, 256)
            scores = mm_nt(jnp.where(mine, queries, 0), keys)
            added = jnp.concatenate(
                [bias[0, h].astype(F32), mm(natural, bias[1, h])], axis=1
            )
            scores = jnp.where(masked, MASKED_SCORE, scores + added)
            scores = scores - jnp.max(scores, axis=1, keepdims=True)
            exps.append(jnp.exp(scores).astype(BF))
            weights.append(
                jnp.concatenate(
                    [jnp.where(mine, values, 0), jnp.where(mine, 1.0, 0.0).astype(BF)], axis=1
                )
            )
        total = total + mm(jnp.concatenate(exps, axis=1), jnp.concatenate(weights, axis=0))
        if g + 2 < 4:
            arrived(g + 2)
    gated = (total[:, 0:256] / total[:, 256:512] * gates).astype(BF)
    m1[...] = (rows + mm(gated, wout[...])).astype(BF).reshape(8, 32, 256)

    for j in (4, 3, 5, 2, 6, 1, 7):
        zp = lax.rem(z + j, 8)
        remote(m1.at[zp], cmid.at[z], ca_s, ca_r, zp * 16 + k).start()
    cmid[z] = m1[z]
    remote(cmid.at[pl.ds(0, 7)], cmid.at[pl.ds(0, 7)], ca_s, ca_r, sib).wait_recv()
    csend[...] = pick(by_k, cmid[...].reshape(256, 256)).reshape(16, 16, 256)
    for j in (8, 7, 9, 6, 10, 5, 11, 4, 12, 3, 13, 2, 14, 1, 15):
        kp = lax.rem(k + j, 16)
        remote(csend.at[kp], out_ref.at[k], cb_s, cb_r, z * 16 + kp).start()
    out_ref[k] = csend[k]
    remote(csend.at[pl.ds(0, 15)], csend.at[pl.ds(0, 15)], cb_s, cb_r, sib).wait_recv()

    remote(xmid.at[pl.ds(0, 15)], xmid.at[pl.ds(0, 15)], xa_s, xa_r, sib).wait_send()
    remote(bmid.at[pl.ds(0, 15)], bmid.at[pl.ds(0, 15)], ba_s, ba_r, sib).wait_send()
    remote(xrows.at[pl.ds(0, 7)], xrows.at[pl.ds(0, 7)], xb_s, xb_r, sib).wait_send()
    for g in range(4):
        part = bias.at[0, pl.ds(2 * g, 2), pl.ds(0, 224)]
        remote(part, part, bb_s.at[g], bb_r.at[g], sib).wait_send()
        part = bias.at[c, pl.ds(2 * g, 2)]
        remote(part, part, dd_s.at[g], dd_r.at[g], sib).wait_send()
    remote(cmid.at[pl.ds(0, 7)], cmid.at[pl.ds(0, 7)], ca_s, ca_r, sib).wait_send()
    remote(csend.at[pl.ds(0, 15)], csend.at[pl.ds(0, 15)], cb_s, cb_r, sib).wait_send()


def column_kernel(
    m_ref, flags_ref, gain_ref, win_ref, wout_ref, tgain_ref, wide_ref, shrink_ref, out_ref
):
    z = lax.axis_index("res") // 16
    apart = selector(lambda o: lax.rem(o, 128) * 2 + o // 128, 256)
    together = selector(lambda o: lax.rem(o, 2) * 128 + o // 2, 256)
    first = mm(apart, m_ref[...])
    normed = normalize(first, gain_ref[...])
    queries = (mm(normed, win_ref[:, 0:256]) * DEPTH ** (-0.5)).astype(BF)
    keys = mm(normed, win_ref[:, 256:512]).astype(BF)
    values = mm(normed, win_ref[:, 512:768]).astype(BF)
    gates = jax.nn.sigmoid(mm(normed, win_ref[:, 768:1024]))
    masked = jnp.where(z // 4 == 0, flags_ref[0:1, :], flags_ref[1:2, :]) == 1
    attended = []
    for r in range(2):
        q, t, v = (a[128 * r : 128 * r + 128] for a in (queries, keys, values))
        exps = []
        weights = []
        for h in range(HEADS):
            mine = head_lanes(h, 128)
            scores = mm_nt(jnp.where(mine, q, 0), t)
            scores = jnp.where(masked, MASKED_SCORE, scores)
            scores = scores - jnp.max(scores, axis=1, keepdims=True)
            exps.append(jnp.exp(scores).astype(BF))
            weights.append(
                jnp.concatenate(
                    [jnp.where(mine, v, 0), jnp.where(mine, 1.0, 0.0).astype(BF)], axis=1
                )
            )
        total = mm(jnp.concatenate(exps, axis=1), jnp.concatenate(weights, axis=0))
        attended.append(total[:, 0:256] / total[:, 256:512])
    gated = (jnp.concatenate(attended, axis=0) * gates).astype(BF)
    second = (first + mm(gated, wout_ref[...])).astype(BF)
    second_f = second.astype(F32)
    hidden = jnp.maximum(mm(normalize(second_f, tgain_ref[...]), wide_ref[...]), 0.0).astype(BF)
    result = (second_f + mm(hidden, shrink_ref[...])).astype(BF)
    out_ref[...] = pick(together, result)


def body(
    aligned_chain_features,
    pair_representation_state,
    gap_block_flags,
    pair_norm_gain,
    pair_head_weight,
    horizontal_scaling_factor,
    row_input_weight,
    horizontal_final_matrix,
    vertical_scaling_factor,
    column_input_weight,
    vertical_final_matrix,
    feedforward_scaling_factor,
    feedforward_widen_matrix,
    feedforward_shrink_matrix,
):
    vmem = pl.BlockSpec(memory_space=pltpu.VMEM)
    hbm = pl.BlockSpec(memory_space=pl.ANY)
    dma = pltpu.SemaphoreType.DMA
    flags = jnp.transpose(gap_block_flags)
    first = pl.pallas_call(
        row_kernel,
        out_shape=jax.ShapeDtypeStruct((16, 16, 256), BF),
        in_specs=[vmem] * 6 + [hbm] * 2,
        out_specs=vmem,
        scratch_shapes=[
            pltpu.VMEM((256, 1024), BF),
            pltpu.VMEM((256, 256), BF),
            pltpu.VMEM((2, 16, 128), BF),
            pltpu.VMEM((16, 16, 256), BF),
            pltpu.VMEM((8, 32, 256), BF),
            pltpu.VMEM((8, 32, 256), BF),
            pltpu.VMEM((16, 16, 128), BF),
            pltpu.VMEM((8, 32, 128), BF),
            pltpu.VMEM((2, 8, 256, 128), BF),
            pltpu.VMEM((8, 32, 256), BF),
            pltpu.VMEM((8, 32, 256), BF),
            pltpu.VMEM((16, 16, 256), BF),
            dma((2,)), dma, dma, dma, dma, dma, dma,
            dma((4,)), dma((4,)), dma((4,)), dma((4,)), dma, dma, dma, dma,
        ],
        name="row_attention",
        compiler_params=pltpu.CompilerParams(
            collective_id=0, has_side_effects=True, vmem_limit_bytes=40 << 20
        ),
    )(
        aligned_chain_features.reshape(16, 16, 256),
        pair_representation_state.reshape(512, 128),
        flags,
        pair_norm_gain.reshape(1, 128),
        jnp.transpose(pair_head_weight),
        horizontal_scaling_factor.reshape(1, 256),
        row_input_weight,
        horizontal_final_matrix,
    )
    result = pl.pallas_call(
        column_kernel,
        out_shape=jax.ShapeDtypeStruct((256, 256), BF),
        in_specs=[vmem] * 8,
        out_specs=vmem,
        name="column_attention",
        compiler_params=pltpu.CompilerParams(vmem_limit_bytes=40 << 20),
    )(
        first.reshape(256, 256),
        flags,
        vertical_scaling_factor.reshape(1, 256),
        column_input_weight,
        vertical_final_matrix,
        feedforward_scaling_factor.reshape(1, 256),
        feedforward_widen_matrix,
        feedforward_shrink_matrix,
    )
    return result.reshape(128, 2, 256)


def solution(mesh):
    placed = (
        P("dp", "res", None),
        P(("dp", "res"), None, None),
        P("dp", None),
        P(),
        P(),
        P(),
        P(),
        P(),
        P(),
        P(),
        P(),
        P(),
        P(),
        P(),
    )
    return jax.shard_map(
        body, mesh=mesh, in_specs=placed, out_specs=P("dp", "res", None), check_vma=False
    )
```

time: 145 us -> 53.3 us (0.37)
  waiting for transfers between devices: 75.6 us -> 0 us
  Pallas kernels: 0 us -> 47.5 us
  starting transfers between devices: 26.7 us -> 0 us
  between operations: 13.7 us -> 0.14 us
  other arithmetic: 12.1 us -> 0 us
  matrix products: 11.1 us -> 0 us
    all_gather x1 -> x0, waiting for transfers between devices: 51.8 us -> none  [body(): bias_all = lax.all_gather(bias_local, 'res', axis=1, tiled=True)]
    pallas_call x0 -> x2, Pallas kernels: none -> 47.5 us  [the longest x1 45 us: body(): pl.pallas_call(row_kernel, out_shape=jax.ShapeDtypeStruct((16, 16, 256),...]
    all_to_all x2 -> x0, starting transfers between devices: 26.7 us -> none  [the longest x1 18.4 us: body(): lax.all_to_all(aligned_chain_features, 'res', split_axis=0, concat_axis=1...]
    all_to_all x2 -> x0, waiting for transfers between devices: 23.9 us -> none  [the longest x1 12.4 us: body(): lax.all_to_all(blocks_out, 'res', split_axis=1, concat_axis=0, tiled=True)]
    dot_general x8 -> x0, matrix products: 8.69 us -> none  [the longest x1 1.85 us: body(): jnp.einsum('ijc,ch->hij', pair_normed, pair_head_weight, preferred_elemen...]
    reduce_sum x7 -> x0, other arithmetic: 6.5 us -> none  [the longest x4 5.09 us: layer_normalize(): spread = jnp.mean(centred * centred, axis=-1, keepdims=True)]
    convert_element_type x4 -> x0, other arithmetic: 3.28 us -> none  [the longest x1 1.55 us: body(): layer_normalize(res_rows, vertical_scaling_factor).astype(jnp.bfloat16)]
    sub x2 -> x0, matrix products: 2.37 us -> none  [the longest x1 1.48 us: body(): col_weights = jax.nn.softmax(col_scores, axis=-1).astype(jnp.bfloat16)]
  transfers between devices with their start and end apart: 3 -> 0, of which waited for: 3 -> 0; matrix products, arithmetic and copies ran while one was open for 3% -> 0% of each run, Pallas kernels for 0% -> 0%
where the time goes in v1:
time: 53.3 us; the launch traced here: 53 us
  Pallas kernels  47.5 us (89%)
  local copies, waits for them, and re-layouts  5.4 us (10%)
    pallas_call x1, Pallas kernels, body(): pl.pallas_call(row_kernel, out_shape=jax.ShapeDtypeStruct((16, 16, 256),...  45 us
    unnamed x26, local copies, waits for them, and re-layouts  3.65 us
    pallas_call x1, Pallas kernels, body(): pl.pallas_call(column_kernel, out_shape=jax.ShapeDtypeStruct((256, 256),...  2.47 us

profile of v1, /device:TPU:1, one launch (start us, length us, event | category | flops | bytes accessed | tf_op | source)
XLA Modules:
  0.0 53.0 jit_solution(12649050191121834563)
XLA Ops:
  0.0 0.0 copy-start.11
  0.0 0.0 copy-start.7
  0.0 0.0 copy-start.8
  0.0 0.0 copy-start.12
  0.0 0.0 copy-start.5
  0.0 0.0 copy-start.4
  0.0 1.0 %reshape.24.x_ref = bf16[16,16,256]{2,1,0:T(8,128)(2,1)S(1)} reshape(bf16[128,2,256]{2,1,0:T(2,128)(2,1)} %param.14) | data formatting | bytes 262144 | tf_op jit(solution)/shard_map/reshape | solution.py:305
  1.1 0.0 copy-done.11
  1.1 0.0 copy-done.7
  1.1 0.0 copy-done.8
  1.1 0.0 copy-done.12
  1.1 0.0 copy-done.5
  1.1 0.0 copy-start
  1.1 1.0 %copy-done = bf16[256,1024]{1,0:T(8,128)(2,1)S(1)} copy-done((bf16[256,1024]{1,0:T(8,128)(2,1)S(1)}, bf16[256,1024]{1,0:T(8,128)(2,1)}, u32[]{:S(2)}) %copy-start) | copy-done | bytes 524312
  2.2 0.0 copy-start.6
  2.2 0.9 %copy-done.6 = bf16[256,256]{1,0:T(8,128)(2,1)S(1)} copy-done((bf16[256,256]{1,0:T(8,128)(2,1)S(1)}, bf16[256,256]{1,0:T(8,128)(2,1)}, u32[]{:S(2)}) %copy-start.6) | copy-done | bytes 131096
  3.1 0.0 copy-start.1
  3.1 0.0 copy-start.2
  3.1 0.0 copy-start.10
  3.1 45.0 %row_attention.1 = bf16[16,16,256]{2,1,0:T(8,128)(2,1)S(1)} custom-call(bf16[16,16,256]{2,1,0:T(8,128)(2,1)S(1)} %reshape.24.x_ref, bf16[512,128]{1,0:T(8,128)(2,1)S(1)} %bitcast.9, s32[2,128]{1,0:T(2,128)S(1)} %bitcast.10, f32[1,128]{1,0:T(1,128)S(1)} %bitcast.16, bf16[8,128]{1,0:T(8,128)(2,1)S(1)} %bitcast.12, f32[1,256]{1,0:T(1,128)S(1)} %bitcast.15, ...), custom_call_target="tpu_custom_call" | custom-call | tf_op jit(solution)/shard_map/row_attention/pallas_call | solution.py:279
  48.1 0.0 copy-start.9
  48.1 0.0 copy-done.4
  48.1 0.0 copy-done.1
  48.1 0.0 copy-done.2
  48.1 0.0 copy-done.10
  48.2 0.6 %copy-done.9 = f32[256]{0:T(256)S(1)} copy-done((f32[256]{0:T(256)S(1)}, f32[256]{0:T(256)}, u32[]{:S(2)}) %copy-start.9) | copy-done | bytes 1048
  48.8 0.0 copy-start.3
  48.8 1.0 %copy-done.3 = bf16[1024,256]{1,0:T(8,128)(2,1)S(1)} copy-done((bf16[1024,256]{1,0:T(8,128)(2,1)S(1)}, bf16[1024,256]{1,0:T(8,128)(2,1)}, u32[]{:S(2)}) %copy-start.3) | copy-done | bytes 524312
  49.8 2.5 %column_attention.1 = bf16[256,256]{1,0:T(8,128)(2,1)S(1)} custom-call(bf16[256,256]{1,0:T(8,128)(2,1)S(1)} %bitcast.8, s32[2,128]{1,0:T(2,128)S(1)} %bitcast.11, f32[1,256]{1,0:T(1,128)S(1)} %bitcast.13, bf16[256,1024]{1,0:T(8,128)(2,1)S(1)} %copy-done.1, bf16[256,256]{1,0:T(8,128)(2,1)S(1)} %copy-done.4, f32[1,256]{1,0:T(1,128)S(1)} %bitcast.14, ...), custom_call_target="tpu_custom_call" | custom-call | tf_op jit(solution)/shard_map/column_attention/pallas_call | solution.py:314
  52.3 0.7 %reshape.31 = bf16[128,2,256]{2,1,0:T(2,128)(2,1)} reshape(bf16[256,256]{1,0:T(8,128)(2,1)S(1)} %column_attention.1) | data formatting | bytes 262144 | tf_op jit(solution)/shard_map/reshape | solution.py:331
Async XLA Ops:
  0.0 1.1 %copy-start.11 = (f32[256]{0:T(256)S(1)}, f32[256]{0:T(256)}, u32[]{:S(2)}) copy-start(f32[256]{0:T(256)} %param.19) | copy-start | bytes 3076
  0.0 1.1 %copy-start.7 = (s32[128,2]{0,1:T(2,128)S(1)}, s32[128,2]{0,1:T(2,128)}, u32[]{:S(2)}) copy-start(s32[128,2]{0,1:T(2,128)} %param.16) | copy-start | bytes 3076
  0.0 1.1 %copy-start.8 = (bf16[128,8]{0,1:T(8,128)(2,1)S(1)}, bf16[128,8]{0,1:T(8,128)(2,1)}, u32[]{:S(2)}) copy-start(bf16[128,8]{0,1:T(8,128)(2,1)} %param.18) | copy-start | bytes 6148
  0.0 1.1 %copy-start.12 = (f32[128]{0:T(128)S(1)}, f32[128]{0:T(128)}, u32[]{:S(2)}) copy-start(f32[128]{0:T(128)} %param.17) | copy-start | bytes 1540
  0.0 1.1 %copy-start.5 = (bf16[2,256,128]{2,1,0:T(8,128)(2,1)S(1)}, bf16[2,256,128]{2,1,0:T(8,128)(2,1)}, u32[]{:S(2)}) copy-start(bf16[2,256,128]{2,1,0:T(8,128)(2,1)} %param.15) | copy-start | bytes 393220
  0.0 48.1 %copy-start.4 = (bf16[256,256]{1,0:T(8,128)(2,1)S(1)}, bf16[256,256]{1,0:T(8,128)(2,1)}, u32[]{:S(2)}) copy-start(bf16[256,256]{1,0:T(8,128)(2,1)} %wout_ref.1) | copy-start | bytes 393220
  1.1 1.0 %copy-start = (bf16[256,1024]{1,0:T(8,128)(2,1)S(1)}, bf16[256,1024]{1,0:T(8,128)(2,1)}, u32[]{:S(2)}) copy-start(bf16[256,1024]{1,0:T(8,128)(2,1)} %win_hbm.1) | copy-start | bytes 1572868
  2.2 0.9 %copy-start.6 = (bf16[256,256]{1,0:T(8,128)(2,1)S(1)}, bf16[256,256]{1,0:T(8,128)(2,1)}, u32[]{:S(2)}) copy-start(bf16[256,256]{1,0:T(8,128)(2,1)} %wout_hbm.1) | copy-start | bytes 393220
  3.1 45.0 %copy-start.1 = (bf16[256,1024]{1,0:T(8,128)(2,1)S(1)}, bf16[256,1024]{1,0:T(8,128)(2,1)}, u32[]{:S(2)}) copy-start(bf16[256,1024]{1,0:T(8,128)(2,1)} %win_ref.1) | copy-start | bytes 1572868
  3.1 45.1 %copy-start.2 = (bf16[256,1024]{1,0:T(8,128)(2,1)S(1)}, bf16[256,1024]{1,0:T(8,128)(2,1)}, u32[]{:S(2)}) copy-start(bf16[256,1024]{1,0:T(8,128)(2,1)} %wide_ref.1) | copy-start | bytes 1572868
  3.1 45.1 %copy-start.10 = (f32[256]{0:T(256)S(1)}, f32[256]{0:T(256)}, u32[]{:S(2)}) copy-start(f32[256]{0:T(256)} %param.25) | copy-start | bytes 3076
  48.1 0.7 %copy-start.9 = (f32[256]{0:T(256)S(1)}, f32[256]{0:T(256)}, u32[]{:S(2)}) copy-start(f32[256]{0:T(256)} %param.22) | copy-start | bytes 3076
  48.8 1.0 %copy-start.3 = (bf16[1024,256]{1,0:T(8,128)(2,1)S(1)}, bf16[1024,256]{1,0:T(8,128)(2,1)}, u32[]{:S(2)}) copy-start(bf16[1024,256]{1,0:T(8,128)(2,1)} %shrink_ref.1) | copy-start | bytes 1572868

commit v2 on v1

v2 whole, which is shorter than its diff:
```python
import jax
import jax.numpy as jnp
from jax import lax
from jax.experimental import pallas as pl
from jax.experimental.pallas import tpu as pltpu
from jax.sharding import PartitionSpec as P

EPSILON = 1e-05
MASKED_SCORE = -1000000000.0
HEADS = 8
DEPTH = 32
BF = jnp.bfloat16
F32 = jnp.float32
MESH = pl.DeviceIdType.MESH
NT = (((1,), (1,)), ((), ()))
FAR_Z = (4, 3, 5, 2, 6, 1, 7)
FAR_K = (8, 7, 9, 6, 10, 5, 11, 4, 12, 3, 13, 2, 14, 1, 15)


def normalize(values, gain):
    centred = values - jnp.mean(values, axis=-1, keepdims=True)
    spread = jnp.mean(centred * centred, axis=-1, keepdims=True)
    return (centred * lax.rsqrt(spread + EPSILON) * gain).astype(BF)


def mm(a, b):
    return jnp.dot(a, b, preferred_element_type=F32)


def mm_nt(a, b):
    return lax.dot_general(a, b, NT, preferred_element_type=F32)


def selector(source_of, rows):
    o = lax.broadcasted_iota(jnp.int32, (rows, rows), 0)
    i = lax.broadcasted_iota(jnp.int32, (rows, rows), 1)
    return jnp.where(source_of(o) == i, 1.0, 0.0).astype(F32).astype(BF)


def pick(one_hot, rows):
    return mm(one_hot, rows).astype(BF)


def head_lanes(h, rows, width=256):
    lane = lax.broadcasted_iota(jnp.int32, (rows, width), 1)
    return lane // DEPTH == h


def value_and_count(mine, values):
    count = jnp.where(mine, 1.0, 0.0).astype(BF)
    return jnp.concatenate([jnp.where(mine, values, 0), count], axis=1)


def remote(src, dst, send, recv, device):
    return pltpu.make_async_remote_copy(
        src_ref=src,
        dst_ref=dst,
        send_sem=send,
        recv_sem=recv,
        device_id={"res": device},
        device_id_type=MESH,
    )


def kernel(
    x_hbm, pair_hbm, flags_hbm, pgain_hbm, pw_hbm, rgain_hbm, rin_hbm, rout_hbm,
    cgain_hbm, cin_hbm, cout_hbm, tgain_hbm, wide_hbm, shrink_hbm,
    out_ref,
    pair, flags, pgain, pw, rgain, rin, rout, cgain, cin, cout, tgain, wide, shrink,
    bloc, xmid, xsend, xrows, bmid, bsend, bias, m1, cmid, csend, cols,
    load_sem, own_sem, xa_s, xa_r, ba_s, ba_r, xb_s, xb_r,
    bb_s, bb_r, dd_s, dd_r, ca_s, ca_r, cb_s, cb_r,
):
    me = lax.axis_index("res")
    z = me // 16
    k = lax.rem(me, 16)
    y = k // 2
    c = lax.rem(me, 2)
    sib = me + 1 - 2 * c

    barrier = pltpu.get_barrier_semaphore()

    def greet(device):
        pl.semaphore_signal(barrier, inc=1, device_id={"res": device}, device_id_type=MESH)

    for j in FAR_Z:
        greet(lax.rem(z + j, 8) * 16 + k)
        greet(lax.rem(z + j, 8) * 16 + y * 2 + 1 - c)
    for j in FAR_K:
        greet(z * 16 + lax.rem(k + j, 16))

    loads = [
        pltpu.make_async_copy(source, target, load_sem.at[n])
        for n, (source, target) in enumerate((
            (pair_hbm, pair), (pgain_hbm, pgain), (pw_hbm, pw), (flags_hbm, flags),
            (rgain_hbm, rgain), (rin_hbm, rin), (rout_hbm, rout),
            (cgain_hbm, cgain), (cin_hbm, cin), (cout_hbm, cout),
            (tgain_hbm, tgain), (wide_hbm, wide), (shrink_hbm, shrink),
        ))
    ]
    for load in loads:
        load.start()
    own = pltpu.make_async_copy(
        x_hbm.at[pl.ds(8 * k, 8)], xmid.at[pl.ds(8 * k, 8)], own_sem
    )
    own.start()

    for load in loads[0:3]:
        load.wait()
    normed = normalize(pair[...].astype(F32), pgain[...])
    biases = mm_nt(pw[...], normed).astype(BF)
    bloc[0] = jnp.concatenate([biases[:, 0:128], biases[:, 256:384]], axis=0)
    bloc[1] = jnp.concatenate([biases[:, 128:256], biases[:, 384:512]], axis=0)

    pl.semaphore_wait(barrier, 29)

    for j in FAR_K:
        kp = lax.rem(k + j, 16)
        remote(
            x_hbm.at[pl.ds(8 * kp, 8)], xmid.at[pl.ds(8 * k, 8)], xa_s, xa_r, z * 16 + kp
        ).start()
    for j in FAR_Z:
        yp = lax.rem(y + j, 8)
        remote(bloc.at[0], bmid.at[k], ba_s, ba_r, z * 16 + yp * 2).start()
        zp = lax.rem(z + j, 8)
        remote(bloc.at[1], bmid.at[z * 2 + c], ba_s, ba_r, zp * 16 + y * 2 + 1).start()

    @pl.when(c == 0)
    def _():
        remote(bloc.at[1], bmid.at[z * 2], ba_s, ba_r, sib).start()
        bmid[k] = bloc[0]

    @pl.when(c == 1)
    def _():
        remote(bloc.at[0], bmid.at[k], ba_s, ba_r, sib).start()
        bmid[z * 2 + 1] = bloc[1]

    by_z = selector(lambda o: lax.rem(o, 32) // 2 * 16 + o // 32 * 2 + lax.rem(o, 2), 256)
    by_h = selector(lambda o: lax.rem(o, 32) // 2 * 16 + lax.rem(o, 2) * 8 + o // 32, 256)
    natural = selector(lambda o: lax.rem(o, 32) // 4 * 32 + o // 32 * 4 + lax.rem(o, 4), 256)

    own.wait()
    remote(xmid.at[pl.ds(0, 120)], xmid.at[pl.ds(0, 120)], xa_s, xa_r, sib).wait_recv()
    xsend[...] = pick(by_z, xmid[...].reshape(256, 256)).reshape(8, 32, 256)
    for j in FAR_Z:
        zp = lax.rem(z + j, 8)
        remote(xsend.at[zp], xrows.at[z], xb_s, xb_r, zp * 16 + k).start()
    xrows[z] = xsend[z]

    remote(bmid.at[pl.ds(0, 15)], bmid.at[pl.ds(0, 15)], ba_s, ba_r, sib).wait_recv()
    bsend[...] = pick(by_h, bmid[...].reshape(256, 128)).reshape(8, 32, 128)
    place = pl.multiple_of(jnp.where(c == 0, z, y) * 32, 32)
    for g in range(4):
        for j in FAR_Z:
            peer = jnp.where(
                c == 0, lax.rem(z + j, 8) * 16 + k, z * 16 + lax.rem(y + j, 8) * 2 + c
            )
            remote(
                bsend.at[pl.ds(2 * g, 2)],
                bias.at[c, pl.ds(2 * g, 2), pl.ds(place, 32)],
                bb_s.at[g],
                bb_r.at[g],
                peer,
            ).start()
    bias[c, :, pl.ds(place, 32), :] = bsend[...]

    def arrived(g):
        part = bias.at[0, pl.ds(2 * g, 2), pl.ds(0, 224)]
        remote(part, part, bb_s.at[g], bb_r.at[g], sib).wait_recv()
        part = bias.at[c, pl.ds(2 * g, 2)]
        remote(part, part, dd_s.at[g], dd_r.at[g], sib).start()

    def complete(g):
        part = bias.at[c, pl.ds(2 * g, 2)]
        remote(part, part, dd_s.at[g], dd_r.at[g], sib).wait_recv()

    for load in loads[3:]:
        load.wait()
    seq = lax.broadcasted_iota(jnp.int32, (2, 128), 1)
    gaps = jnp.sum(jnp.where(seq == 8 * k + z, flags[...], 0), axis=1, keepdims=True)
    half = lax.broadcasted_iota(jnp.int32, (1, 256), 1) // 128
    masked = jnp.where(half == 0, gaps[0:1], gaps[1:2]) == 1

    remote(xrows.at[pl.ds(0, 7)], xrows.at[pl.ds(0, 7)], xb_s, xb_r, sib).wait_recv()
    rows = xrows[...].reshape(256, 256).astype(F32)
    row_normed = normalize(rows, rgain[...])
    queries = (mm(row_normed, rin[:, 0:256]) * DEPTH ** (-0.5)).astype(BF)
    keys = mm(row_normed, rin[:, 256:512]).astype(BF)
    values = mm(row_normed, rin[:, 512:768]).astype(BF)
    gates = jax.nn.sigmoid(mm(row_normed, rin[:, 768:1024]))

    arrived(0)
    arrived(1)
    total = jnp.zeros((256, 512), F32)
    for g in range(4):
        complete(g)
        exps = []
        weights = []
        for h in (2 * g, 2 * g + 1):
            mine = head_lanes(h, 256)
            scores = mm_nt(jnp.where(mine, queries, 0), keys)
            added = jnp.concatenate(
                [bias[0, h].astype(F32), mm(natural, bias[1, h])], axis=1
            )
            scores = jnp.where(masked, MASKED_SCORE, scores + added)
            scores = scores - jnp.max(scores, axis=1, keepdims=True)
            exps.append(jnp.exp(scores).astype(BF))
            weights.append(value_and_count(mine, values))
        total = total + mm(jnp.concatenate(exps, axis=1), jnp.concatenate(weights, axis=0))
        if g + 2 < 4:
            arrived(g + 2)
    gated = (total[:, 0:256] / total[:, 256:512] * gates).astype(BF)
    m1[...] = (rows + mm(gated, rout[...])).astype(BF).reshape(8, 32, 256)

    for j in FAR_Z:
        zp = lax.rem(z + j, 8)
        remote(m1.at[zp], cmid.at[z], ca_s, ca_r, zp * 16 + k).start()
    cmid[z] = m1[z]
    by_k = selector(lambda o: lax.rem(o, 16) // 2 * 32 + o // 16 * 2 + lax.rem(o, 2), 256)
    apart = selector(lambda o: lax.rem(o, 128) * 2 + o // 128, 256)
    together = selector(lambda o: lax.rem(o, 2) * 128 + o // 2, 256)
    masked = jnp.where(z // 4 == 0, flags[0:1, :], flags[1:2, :]) == 1
    remote(cmid.at[pl.ds(0, 7)], cmid.at[pl.ds(0, 7)], ca_s, ca_r, sib).wait_recv()
    csend[...] = pick(by_k, cmid[...].reshape(256, 256)).reshape(16, 16, 256)
    for j in FAR_K:
        kp = lax.rem(k + j, 16)
        remote(csend.at[kp], cols.at[k], cb_s, cb_r, z * 16 + kp).start()
    cols[k] = csend[k]
    remote(csend.at[pl.ds(0, 15)], csend.at[pl.ds(0, 15)], cb_s, cb_r, sib).wait_recv()

    first = mm(apart, cols[...].reshape(256, 256))
    normed = normalize(first, cgain[...])
    queries = (mm(normed, cin[:, 0:256]) * DEPTH ** (-0.5)).astype(BF)
    keys = mm(normed, cin[:, 256:512]).astype(BF)
    values = mm(normed, cin[:, 512:768]).astype(BF)
    gates = jax.nn.sigmoid(mm(normed, cin[:, 768:1024]))
    attended = []
    for r in range(2):
        q, t, v = (a[128 * r : 128 * r + 128] for a in (queries, keys, values))
        exps = []
        weights = []
        for h in range(HEADS):
            mine = head_lanes(h, 128)
            scores = mm_nt(jnp.where(mine, q, 0), t)
            scores = jnp.where(masked, MASKED_SCORE, scores)
            scores = scores - jnp.max(scores, axis=1, keepdims=True)
            exps.append(jnp.exp(scores).astype(BF))
            weights.append(value_and_count(mine, v))
        total = mm(jnp.concatenate(exps, axis=1), jnp.concatenate(weights, axis=0))
        attended.append(total[:, 0:256] / total[:, 256:512])
    gated = (jnp.concatenate(attended, axis=0) * gates).astype(BF)
    second = (first + mm(gated, cout[...])).astype(BF).astype(F32)
    hidden = jnp.maximum(mm(normalize(second, tgain[...]), wide[...]), 0.0).astype(BF)
    result = (second + mm(hidden, shrink[...])).astype(BF)
    out_ref[...] = pick(together, result).reshape(128, 2, 256)

    remote(xmid.at[pl.ds(0, 120)], xmid.at[pl.ds(0, 120)], xa_s, xa_r, sib).wait_send()
    remote(bmid.at[pl.ds(0, 15)], bmid.at[pl.ds(0, 15)], ba_s, ba_r, sib).wait_send()
    remote(xrows.at[pl.ds(0, 7)], xrows.at[pl.ds(0, 7)], xb_s, xb_r, sib).wait_send()
    for g in range(4):
        part = bias.at[0, pl.ds(2 * g, 2), pl.ds(0, 224)]
        remote(part, part, bb_s.at[g], bb_r.at[g], sib).wait_send()
        part = bias.at[c, pl.ds(2 * g, 2)]
        remote(part, part, dd_s.at[g], dd_r.at[g], sib).wait_send()
    remote(cmid.at[pl.ds(0, 7)], cmid.at[pl.ds(0, 7)], ca_s, ca_r, sib).wait_send()
    remote(csend.at[pl.ds(0, 15)], csend.at[pl.ds(0, 15)], cb_s, cb_r, sib).wait_send()


def body(
    aligned_chain_features,
    pair_representation_state,
    gap_block_flags,
    pair_norm_gain,
    pair_head_weight,
    horizontal_scaling_factor,
    row_input_weight,
    horizontal_final_matrix,
    vertical_scaling_factor,
    column_input_weight,
    vertical_final_matrix,
    feedforward_scaling_factor,
    feedforward_widen_matrix,
    feedforward_shrink_matrix,
):
    dma = pltpu.SemaphoreType.DMA
    operands = (
        aligned_chain_features,
        pair_representation_state.reshape(512, 128),
        jnp.transpose(gap_block_flags),
        pair_norm_gain.reshape(1, 128),
        jnp.transpose(pair_head_weight),
        horizontal_scaling_factor.reshape(1, 256),
        row_input_weight,
        horizontal_final_matrix,
        vertical_scaling_factor.reshape(1, 256),
        column_input_weight,
        vertical_final_matrix,
        feedforward_scaling_factor.reshape(1, 256),
        feedforward_widen_matrix,
        feedforward_shrink_matrix,
    )
    return pl.pallas_call(
        kernel,
        out_shape=jax.ShapeDtypeStruct((128, 2, 256), BF),
        in_specs=[pl.BlockSpec(memory_space=pl.ANY)] * len(operands),
        out_specs=pl.BlockSpec(memory_space=pltpu.VMEM),
        scratch_shapes=[pltpu.VMEM(a.shape, a.dtype) for a in operands[1:]]
        + [
            pltpu.VMEM((2, 16, 128), BF),
            pltpu.VMEM((128, 2, 256), BF),
            pltpu.VMEM((8, 32, 256), BF),
            pltpu.VMEM((8, 32, 256), BF),
            pltpu.VMEM((16, 16, 128), BF),
            pltpu.VMEM((8, 32, 128), BF),
            pltpu.VMEM((2, 8, 256, 128), BF),
            pltpu.VMEM((8, 32, 256), BF),
            pltpu.VMEM((8, 32, 256), BF),
            pltpu.VMEM((16, 16, 256), BF),
            pltpu.VMEM((16, 16, 256), BF),
            dma((13,)), dma, dma, dma, dma, dma, dma, dma,
            dma((4,)), dma((4,)), dma((4,)), dma((4,)), dma, dma, dma, dma,
        ],
        name="evoformer",
        compiler_params=pltpu.CompilerParams(
            collective_id=0, has_side_effects=True, vmem_limit_bytes=56 << 20
        ),
    )(*operands)


def solution(mesh):
    placed = (
        P("dp", "res", None),
        P(("dp", "res"), None, None),
        P("dp", None),
        P(),
        P(),
        P(),
        P(),
        P(),
        P(),
        P(),
        P(),
        P(),
        P(),
        P(),
    )
    return jax.shard_map(
        body, mesh=mesh, in_specs=placed, out_specs=P("dp", "res", None), check_vma=False
    )
```

time: 53.3 us -> 49.8 us (0.934)
  local copies, waits for them, and re-layouts: 5.4 us -> 1.65 us
    unnamed x26 -> x1, local copies, waits for them, and re-layouts: 3.65 us -> 1.65 us
    reshape x2 -> x0, local copies, waits for them, and re-layouts: 1.75 us -> none  [the longest x1 1.03 us: body(): aligned_chain_features.reshape(16, 16, 256)]
    pallas_call x2 -> x1, Pallas kernels: 47.5 us -> 48 us  [body(): pl.pallas_call(kernel, out_shape=jax.ShapeDtypeStruct((128, 2, 256), BF),...]
where the time goes in v2:
time: 49.8 us; the launch traced here: 49.7 us
  Pallas kernels  48 us (96%)
  local copies, waits for them, and re-layouts  1.65 us (3%)
    pallas_call x1, Pallas kernels, body(): pl.pallas_call(kernel, out_shape=jax.ShapeDtypeStruct((128, 2, 256), BF),...  48 us
    unnamed x1, local copies, waits for them, and re-layouts  1.65 us

profile of v2, /device:TPU:1, one launch (start us, length us, event | category | flops | bytes accessed | tf_op | source)
XLA Modules:
  0.0 49.7 jit_solution(14029826410030490424)
XLA Ops:
  0.0 48.0 %evoformer.1 = bf16[128,2,256]{2,1,0:T(2,128)(2,1)} custom-call(bf16[128,2,256]{2,1,0:T(2,128)(2,1)} %x_hbm.1, bf16[512,128]{1,0:T(8,128)(2,1)} %bitcast.7, s32[2,128]{1,0:T(2,128)} %bitcast.9, f32[1,128]{1,0:T(1,128)} %bitcast.13, bf16[8,128]{1,0:T(8,128)(2,1)} %bitcast.8, f32[1,256]{1,0:T(1,128)} %bitcast.10, bf16[256,1024]{1,0:T(8,128)(2,1)} %rin_hbm.1, ...), custom_call_target="tpu_custom_call" | custom-call | tf_op jit(solution)/shard_map/evoformer/pallas_call | solution.py:302
  48.0 1.7 %copy.16 = bf16[128,2,256]{2,1,0:T(2,128)(2,1)} copy(bf16[128,2,256]{2,1,0:T(2,128)(2,1)} %evoformer.1) | data formatting | bytes 262144

commit v3 on v2

v3 whole, which is shorter than its diff:
```python
import jax
import jax.numpy as jnp
from jax import lax
from jax.experimental import pallas as pl
from jax.experimental.pallas import tpu as pltpu
from jax.sharding import PartitionSpec as P

EPSILON = 1e-05
MASKED_SCORE = -1000000000.0
HEADS = 8
DEPTH = 32
BF = jnp.bfloat16
F32 = jnp.float32
MESH = pl.DeviceIdType.MESH
NT = (((1,), (1,)), ((), ()))
FAR_Z = (4, 3, 5, 2, 6, 1, 7)
FAR = sorted(
    [(dz, dy, dc) for dz in range(8) for dy in range(8) for dc in range(2)][1:],
    key=lambda d: -min(d[0], 8 - d[0]) - min(d[1], 8 - d[1]),
)
FAR_K = (8, 7, 9, 6, 10, 5, 11, 4, 12, 3, 13, 2, 14, 1, 15)


def normalize(values, gain):
    centred = values - jnp.mean(values, axis=-1, keepdims=True)
    spread = jnp.mean(centred * centred, axis=-1, keepdims=True)
    return (centred * lax.rsqrt(spread + EPSILON) * gain).astype(BF)


def mm(a, b):
    return jnp.dot(a, b, preferred_element_type=F32)


def mm_nt(a, b):
    return lax.dot_general(a, b, NT, preferred_element_type=F32)


def selector(source_of, rows):
    o = lax.broadcasted_iota(jnp.int32, (rows, rows), 0)
    i = lax.broadcasted_iota(jnp.int32, (rows, rows), 1)
    return jnp.where(source_of(o) == i, 1.0, 0.0).astype(F32).astype(BF)


def pick(one_hot, rows):
    return mm(one_hot, rows).astype(BF)


def head_lanes(h, rows, width=128):
    lane = lax.broadcasted_iota(jnp.int32, (rows, width), 1)
    return lane // DEPTH == h


def value_and_count(mine, values):
    count = jnp.where(mine, 1.0, 0.0).astype(BF)
    return jnp.concatenate([jnp.where(mine, values, 0), count], axis=1)


def remote(src, dst, send, recv, device):
    return pltpu.make_async_remote_copy(
        src_ref=src,
        dst_ref=dst,
        send_sem=send,
        recv_sem=recv,
        device_id={"res": device},
        device_id_type=MESH,
    )


def kernel(
    x_hbm, pair_hbm, flags_hbm, pgain_hbm, pw_hbm, rgain_hbm, rin_hbm, rout_hbm,
    cgain_hbm, cin_hbm, cout_hbm, tgain_hbm, wide_hbm, shrink_hbm,
    out_ref,
    pair, flags, pgain, pw, rgain, rin, rout, cgain, cin, cout, tgain, wide, shrink,
    bloc, bmid, bsend, bias, xloc, xmid, xsend, xrows, gsend, cols,
    load_sem, rin_sem, own_sem, ba_s, ba_r, bb_s, bb_r, xa_s, xa_r, xb_s, xb_r,
    xd_s, xd_r, g_s, g_r,
):
    me = lax.axis_index("res")
    z = me // 16
    k = lax.rem(me, 16)
    y = k // 2
    c = lax.rem(me, 2)
    sib = me + 1 - 2 * c

    barrier = pltpu.get_barrier_semaphore()

    def greet(device):
        pl.semaphore_signal(barrier, inc=1, device_id={"res": device}, device_id_type=MESH)

    for j in FAR_Z:
        greet(lax.rem(z + j, 8) * 16 + k)
        greet(lax.rem(z + j, 8) * 16 + y * 2 + 1 - c)
    for j in FAR_K:
        greet(z * 16 + lax.rem(k + j, 16))

    loads = [
        pltpu.make_async_copy(source, target, load_sem.at[n])
        for n, (source, target) in enumerate((
            (pair_hbm, pair), (pgain_hbm, pgain), (pw_hbm, pw), (flags_hbm, flags),
            (rgain_hbm, rgain), (rout_hbm, rout),
            (cgain_hbm, cgain), (cin_hbm, cin), (cout_hbm, cout),
            (tgain_hbm, tgain), (wide_hbm, wide), (shrink_hbm, shrink), (x_hbm, xloc),
        ))
    ]
    loads += [
        pltpu.make_async_copy(
            rin_hbm.at[:, pl.ds(pl.multiple_of(t * 256 + c * 128, 128), 128)],
            rin.at[t],
            rin_sem.at[t],
        )
        for t in range(4)
    ]
    for load in loads:
        load.start()
    own = pltpu.make_async_copy(
        x_hbm.at[pl.ds(8 * k, 8)], xmid.at[pl.ds(8 * k, 8)], own_sem.at[0]
    )
    own.start()

    for load in loads[0:3]:
        load.wait()
    normed = normalize(pair[...].astype(F32), pgain[...])
    biases = mm_nt(pw[...], normed)
    for group in range(2):
        heads = biases[4 * group : 4 * group + 4]
        bloc[group] = jnp.concatenate(
            [heads[:, 128 * n : 128 * n + 128] for n in range(4)], axis=0
        ).astype(BF)

    pl.semaphore_wait(barrier, 29)

    for j in FAR_Z:
        yp = lax.rem(y + j, 8)
        remote(bloc.at[0], bmid.at[k], ba_s, ba_r, z * 16 + yp * 2).start()
        zp = lax.rem(z + j, 8)
        remote(bloc.at[1], bmid.at[z * 2 + c], ba_s, ba_r, zp * 16 + y * 2 + 1).start()

    @pl.when(c == 0)
    def _():
        remote(bloc.at[1], bmid.at[z * 2], ba_s, ba_r, sib).start()
        bmid[k] = bloc[0]

    @pl.when(c == 1)
    def _():
        remote(bloc.at[0], bmid.at[k], ba_s, ba_r, sib).start()
        bmid[z * 2 + 1] = bloc[1]

    for j in FAR_K:
        kp = lax.rem(k + j, 16)
        remote(
            x_hbm.at[pl.ds(8 * kp, 8)], xmid.at[pl.ds(8 * k, 8)], xa_s, xa_r, z * 16 + kp
        ).start()

    by_h = selector(
        lambda o: lax.rem(o, 32) // 2 * 16 + lax.rem(o, 2) * 8 + o // 128 * 4
        + lax.rem(o, 128) // 32,
        256,
    )
    by_z = selector(lambda o: lax.rem(o, 32) // 2 * 16 + o // 32 * 2 + lax.rem(o, 2), 256)
    natural = selector(
        lambda o: jnp.where(c == 0, o, lax.rem(o, 32) // 4 * 32 + o // 32 * 4 + lax.rem(o, 4)),
        256,
    )

    def spread(g):
        for j in FAR_Z:
            peer = jnp.where(
                c == 0, lax.rem(z + j, 8) * 16 + k, z * 16 + lax.rem(y + j, 8) * 2 + c
            )
            remote(
                bsend.at[g], bias.at[g, pl.ds(place, 32)], bb_s.at[g], bb_r.at[g], peer
            ).start()

    place = pl.multiple_of(jnp.where(c == 0, z, y) * 32, 32)
    remote(bmid.at[pl.ds(0, 15)], bmid.at[pl.ds(0, 15)], ba_s, ba_r, sib).wait_recv()
    sorted_bias = pick(by_h, bmid[...].reshape(256, 128))
    bsend[...] = jnp.concatenate([sorted_bias[0:128], sorted_bias[128:256]], axis=1).reshape(
        4, 32, 256
    )
    spread(0)

    own.wait()
    remote(xmid.at[pl.ds(0, 120)], xmid.at[pl.ds(0, 120)], xa_s, xa_r, sib).wait_recv()
    xsend[...] = pick(by_z, xmid[...].reshape(256, 256)).reshape(8, 32, 256)
    for j in FAR_Z:
        zp = lax.rem(z + j, 8)
        remote(xsend.at[zp], xrows.at[c, z], xb_s, xb_r, zp * 16 + k).start()
    xrows[c, z] = xsend[z]
    for g in range(1, 4):
        spread(g)
    bias[:, pl.ds(place, 32), :] = bsend[...]

    for load in loads[3:]:
        load.wait()
    seq = lax.broadcasted_iota(jnp.int32, (2, 128), 1)
    half = lax.broadcasted_iota(jnp.int32, (1, 256), 1) // 128
    masks = []
    for q in range(2):
        gaps = jnp.sum(
            jnp.where(seq == 16 * y + 8 * q + z, flags[...], 0), axis=1, keepdims=True
        )
        masks.append(jnp.where(half == 0, gaps[0:1], gaps[1:2]) == 1)

    got = xrows.at[c, pl.ds(0, 7)]
    remote(got, got, xb_s, xb_r, sib).wait_recv()
    swap = remote(xrows.at[c], xrows.at[c], xd_s, xd_r, sib)
    swap.start()
    swap.wait_recv()
    row_normed = normalize(xrows[...].reshape(512, 256).astype(F32), rgain[...])
    queries = (mm(row_normed, rin[0]) * DEPTH ** (-0.5)).astype(BF)
    keys = mm(row_normed, rin[1]).astype(BF)
    values = mm(row_normed, rin[2]).astype(BF)
    gates = jax.nn.sigmoid(mm(row_normed, rin[3]))

    totals = [jnp.zeros((256, 256), F32)] * 2
    for g in range(4):
        part = bias.at[g, pl.ds(0, 224)]
        remote(part, part, bb_s.at[g], bb_r.at[g], sib).wait_recv()
        added = mm(natural, bias[g])
        mine = head_lanes(g, 256)
        for q in range(2):
            here = slice(256 * q, 256 * q + 256)
            scores = mm_nt(jnp.where(mine, queries[here], 0), keys[here]) + added
            scores = jnp.where(masks[q], MASKED_SCORE, scores)
            scores = scores - jnp.max(scores, axis=1, keepdims=True)
            totals[q] = totals[q] + mm(
                jnp.exp(scores).astype(BF), value_and_count(mine, values[here])
            )
    for q in range(2):
        gated = totals[q][:, 0:128] / totals[q][:, 128:256] * gates[256 * q : 256 * q + 256]
        gsend[q] = gated.astype(BF).reshape(128, 2, 128)

    lanes = pl.ds(pl.multiple_of(c * 128, 128), 128)
    keep = pltpu.make_async_copy(
        gsend.at[:, me], cols.at[y, :, z, :, lanes], own_sem.at[1]
    )
    keep.start()
    for dz, dy, dc in FAR:
        peer = lax.rem(z + dz, 8) * 16 + lax.rem(y + dy, 8) * 2 + (c if dc == 0 else 1 - c)
        remote(gsend.at[:, peer], cols.at[y, :, z, :, lanes], g_s, g_r, peer).start()

    apart = selector(lambda o: lax.rem(o, 128) * 2 + o // 128, 256)
    together = selector(lambda o: lax.rem(o, 2) * 128 + o // 2, 256)
    masked = jnp.where(z // 4 == 0, flags[0:1, :], flags[1:2, :]) == 1
    residual = mm(apart, xloc[...].reshape(256, 256))
    keep.wait()
    got = gsend.at[:, pl.ds(0, 127)]
    remote(got, got, g_s, g_r, sib).wait_recv()

    gated = pick(apart, cols[...].reshape(256, 256))
    first = (residual + mm(gated, rout[...])).astype(BF).astype(F32)
    normed = normalize(first, cgain[...])
    queries = (mm(normed, cin[:, 0:256]) * DEPTH ** (-0.5)).astype(BF)
    keys = mm(normed, cin[:, 256:512]).astype(BF)
    values = mm(normed, cin[:, 512:768]).astype(BF)
    gates = jax.nn.sigmoid(mm(normed, cin[:, 768:1024]))
    attended = []
    for r in range(2):
        q, t, v = (a[128 * r : 128 * r + 128] for a in (queries, keys, values))
        exps = []
        weights = []
        for h in range(HEADS):
            mine = head_lanes(h, 128, 256)
            scores = mm_nt(jnp.where(mine, q, 0), t)
            scores = jnp.where(masked, MASKED_SCORE, scores)
            scores = scores - jnp.max(scores, axis=1, keepdims=True)
            exps.append(jnp.exp(scores).astype(BF))
            weights.append(value_and_count(mine, v))
        total = mm(jnp.concatenate(exps, axis=1), jnp.concatenate(weights, axis=0))
        attended.append(total[:, 0:256] / total[:, 256:512])
    gated = (jnp.concatenate(attended, axis=0) * gates).astype(BF)
    second = (first + mm(gated, cout[...])).astype(BF).astype(F32)
    hidden = jnp.maximum(mm(normalize(second, tgain[...]), wide[...]), 0.0).astype(BF)
    result = (second + mm(hidden, shrink[...])).astype(BF)
    out_ref[...] = pick(together, result)

    remote(bmid.at[pl.ds(0, 15)], bmid.at[pl.ds(0, 15)], ba_s, ba_r, sib).wait_send()
    remote(xmid.at[pl.ds(0, 120)], xmid.at[pl.ds(0, 120)], xa_s, xa_r, sib).wait_send()
    got = xrows.at[c, pl.ds(0, 7)]
    remote(got, got, xb_s, xb_r, sib).wait_send()
    swap.wait_send()
    for g in range(4):
        part = bias.at[g, pl.ds(0, 224)]
        remote(part, part, bb_s.at[g], bb_r.at[g], sib).wait_send()
    got = gsend.at[:, pl.ds(0, 127)]
    remote(got, got, g_s, g_r, sib).wait_send()


def body(
    aligned_chain_features,
    pair_representation_state,
    gap_block_flags,
    pair_norm_gain,
    pair_head_weight,
    horizontal_scaling_factor,
    row_input_weight,
    horizontal_final_matrix,
    vertical_scaling_factor,
    column_input_weight,
    vertical_final_matrix,
    feedforward_scaling_factor,
    feedforward_widen_matrix,
    feedforward_shrink_matrix,
):
    dma = pltpu.SemaphoreType.DMA
    operands = (
        aligned_chain_features,
        pair_representation_state.reshape(512, 128),
        jnp.transpose(gap_block_flags),
        pair_norm_gain.reshape(1, 128),
        jnp.transpose(pair_head_weight),
        horizontal_scaling_factor.reshape(1, 256),
        row_input_weight,
        horizontal_final_matrix,
        vertical_scaling_factor.reshape(1, 256),
        column_input_weight,
        vertical_final_matrix,
        feedforward_scaling_factor.reshape(1, 256),
        feedforward_widen_matrix,
        feedforward_shrink_matrix,
    )
    copies = [a.shape for a in operands[1:]]
    copies[5] = (4, 256, 128)
    result = pl.pallas_call(
        kernel,
        out_shape=jax.ShapeDtypeStruct((256, 256), BF),
        in_specs=[pl.BlockSpec(memory_space=pl.ANY)] * len(operands),
        out_specs=pl.BlockSpec(memory_space=pltpu.VMEM),
        scratch_shapes=[pltpu.VMEM(n, a.dtype) for n, a in zip(copies, operands[1:])]
        + [
            pltpu.VMEM((2, 16, 128), BF),
            pltpu.VMEM((16, 16, 128), BF),
            pltpu.VMEM((4, 32, 256), BF),
            pltpu.VMEM((4, 256, 256), BF),
            pltpu.VMEM((128, 2, 256), BF),
            pltpu.VMEM((128, 2, 256), BF),
            pltpu.VMEM((8, 32, 256), BF),
            pltpu.VMEM((2, 8, 32, 256), BF),
            pltpu.VMEM((2, 128, 2, 128), BF),
            pltpu.VMEM((8, 2, 8, 2, 256), BF),
            dma((13,)), dma((4,)), dma((2,)), dma, dma, dma((4,)), dma((4,)),
            dma, dma, dma, dma, dma, dma, dma, dma,
        ],
        name="evoformer",
        compiler_params=pltpu.CompilerParams(
            collective_id=0, has_side_effects=True, vmem_limit_bytes=56 << 20
        ),
    )(*operands)
    return result.reshape(128, 2, 256)


def solution(mesh):
    placed = (
        P("dp", "res", None),
        P(("dp", "res"), None, None),
        P("dp", None),
        P(),
        P(),
        P(),
        P(),
        P(),
        P(),
        P(),
        P(),
        P(),
        P(),
        P(),
    )
    return jax.shard_map(
        body, mesh=mesh, in_specs=placed, out_specs=P("dp", "res", None), check_vma=False
    )
```

time: 49.8 us -> 43.7 us (0.88)
  Pallas kernels: 48 us -> 41.9 us
    pallas_call x1, Pallas kernels: 48 us -> 41.9 us  [body(): pl.pallas_call(kernel, out_shape=jax.ShapeDtypeStruct((256, 256), BF), in...]
    unnamed x1 -> x0, local copies, waits for them, and re-layouts: 1.65 us -> none
    reshape x0 -> x1, local copies, waits for them, and re-layouts: none -> 1.62 us  [body(): return result.reshape(128, 2, 256)]
where the time goes in v3:
time: 43.7 us; the launch traced here: 43.5 us
  Pallas kernels  41.9 us (96%)
  local copies, waits for them, and re-layouts  1.62 us (4%)
    pallas_call x1, Pallas kernels, body(): pl.pallas_call(kernel, out_shape=jax.ShapeDtypeStruct((256, 256), BF), in...  41.9 us
    reshape x1, local copies, waits for them, and re-layouts, body(): return result.reshape(128, 2, 256)  1.62 us

profile of v3, /device:TPU:1, one launch (start us, length us, event | category | flops | bytes accessed | tf_op | source)
XLA Modules:
  0.0 43.5 jit_solution(1618110735544903212)
XLA Ops:
  0.0 41.9 %evoformer.1 = bf16[256,256]{1,0:T(8,128)(2,1)} custom-call(bf16[128,2,256]{2,1,0:T(2,128)(2,1)} %x_hbm.1, bf16[512,128]{1,0:T(8,128)(2,1)} %bitcast.7, s32[2,128]{1,0:T(2,128)} %bitcast.9, f32[1,128]{1,0:T(1,128)} %bitcast.13, bf16[8,128]{1,0:T(8,128)(2,1)} %bitcast.8, f32[1,256]{1,0:T(1,128)} %bitcast.10, bf16[256,1024]{1,0:T(8,128)(2,1)} %rin_hbm.1, ...), custom_call_target="tpu_custom_call" | custom-call | tf_op jit(solution)/shard_map/evoformer/pallas_call | solution.py:324
  41.9 1.6 %reshape.23 = bf16[128,2,256]{2,1,0:T(2,128)(2,1)} reshape(bf16[256,256]{1,0:T(8,128)(2,1)} %evoformer.1) | data formatting | bytes 262144 | tf_op jit(solution)/shard_map/reshape | solution.py:349

commit v4 on v3

v4 whole, which is shorter than its diff:
```python
import jax
import jax.numpy as jnp
from jax import lax
from jax.experimental import pallas as pl
from jax.experimental.pallas import tpu as pltpu
from jax.sharding import PartitionSpec as P

EPSILON = 1e-05
MASKED_SCORE = -1000000000.0
HEADS = 8
DEPTH = 32
BF = jnp.bfloat16
F32 = jnp.float32
MESH = pl.DeviceIdType.MESH
NT = (((1,), (1,)), ((), ()))
FAR_Z = (4, 3, 5, 2, 6, 1, 7)
FAR_K = (8, 7, 9, 6, 10, 5, 11, 4, 12, 3, 13, 2, 14, 1, 15)


def normalize(values, gain):
    centred = values - jnp.mean(values, axis=-1, keepdims=True)
    spread = jnp.mean(centred * centred, axis=-1, keepdims=True)
    return (centred * lax.rsqrt(spread + EPSILON) * gain).astype(BF)


def mm(a, b):
    return jnp.dot(a, b, preferred_element_type=F32)


def mm_nt(a, b):
    return lax.dot_general(a, b, NT, preferred_element_type=F32)


def selector(source_of, rows):
    o = lax.broadcasted_iota(jnp.int32, (rows, rows), 0)
    i = lax.broadcasted_iota(jnp.int32, (rows, rows), 1)
    return jnp.where(source_of(o) == i, 1.0, 0.0).astype(F32).astype(BF)


def pick(one_hot, rows):
    return mm(one_hot, rows).astype(BF)


def head_lanes(h, rows, width=128):
    lane = lax.broadcasted_iota(jnp.int32, (rows, width), 1)
    return lane // DEPTH == h


def value_and_count(mine, values):
    count = jnp.where(mine, 1.0, 0.0).astype(BF)
    return jnp.concatenate([jnp.where(mine, values, 0), count], axis=1)


def remote(src, dst, send, recv, device):
    return pltpu.make_async_remote_copy(
        src_ref=src,
        dst_ref=dst,
        send_sem=send,
        recv_sem=recv,
        device_id={"res": device},
        device_id_type=MESH,
    )


def kernel(
    x_hbm, pair_hbm, flags_hbm, pgain_hbm, pw_hbm, rgain_hbm, rin_hbm, rout_hbm,
    cgain_hbm, cin_hbm, cout_hbm, tgain_hbm, wide_hbm, shrink_hbm,
    out_ref,
    xloc, pair, flags, pgain, pw, rgain, rin, rout, cgain, cin, cout, tgain, wide, shrink,
    bloc, bmid, bsend, bias, xgo, xmid, xsend, xrows, query, gate, gsend, cols,
    load_sem, rin_sem, own_sem, ba_s, ba_r, bb_s, bb_r, xa_s, xa_r, xb_s, xb_r,
    xd_s, xd_r, g_s, g_r,
):
    me = lax.axis_index("res")
    z = me // 16
    k = lax.rem(me, 16)
    y = k // 2
    c = lax.rem(me, 2)
    sib = me + 1 - 2 * c
    place = jnp.where(c == 0, z, y)
    slot = jnp.where(c == 0, y, z)
    line = slot * 2 + c

    def device(p, n):
        return jnp.where(c == 0, p * 16 + n, n // 2 * 16 + p * 2 + lax.rem(n, 2))

    barrier = pltpu.get_barrier_semaphore()

    def greet(peer):
        pl.semaphore_signal(barrier, inc=1, device_id={"res": peer}, device_id_type=MESH)

    for j in FAR_Z:
        greet(lax.rem(z + j, 8) * 16 + k)
        greet(z * 16 + lax.rem(y + j, 8) * 2 + c)
        greet(lax.rem(z + j, 8) * 16 + y * 2 + 1 - c)
        greet(z * 16 + lax.rem(y + j, 8) * 2 + 1 - c)
    greet(sib)

    loads = [
        pltpu.make_async_copy(source, target, load_sem.at[n])
        for n, (source, target) in enumerate((
            (pair_hbm, pair), (pgain_hbm, pgain), (pw_hbm, pw), (x_hbm, xloc),
            (flags_hbm, flags), (rgain_hbm, rgain), (rout_hbm, rout),
            (cgain_hbm, cgain), (cin_hbm, cin), (cout_hbm, cout),
            (tgain_hbm, tgain), (wide_hbm, wide), (shrink_hbm, shrink),
        ))
    ]
    loads += [
        pltpu.make_async_copy(
            rin_hbm.at[:, pl.ds(pl.multiple_of(t * 256 + c * 128, 128), 128)],
            rin.at[t],
            rin_sem.at[t],
        )
        for t in range(4)
    ]
    for load in loads:
        load.start()

    for load in loads[0:3]:
        load.wait()
    normed = normalize(pair[...].astype(F32), pgain[...])
    biases = mm_nt(pw[...], normed)
    for group in range(2):
        heads = biases[4 * group : 4 * group + 4]
        bloc[group] = jnp.concatenate(
            [heads[:, 128 * n : 128 * n + 128] for n in range(4)], axis=0
        ).astype(BF)
    by_n = selector(
        lambda o: device(lax.rem(o, 16) // 2, o // 16) * 2 + lax.rem(o, 2), 256
    )
    loads[3].wait()
    xgo[...] = pick(by_n, xloc[...].reshape(256, 256)).reshape(16, 16, 256)

    pl.semaphore_wait(barrier, 29)

    for j in FAR_K:
        n = lax.rem(line + j, 16)
        remote(xgo.at[n], xmid.at[c, slot], xa_s, xa_r, device(place, n)).start()
    for j in FAR_Z:
        yp = lax.rem(y + j, 8)
        remote(bloc.at[0], bmid.at[k], ba_s, ba_r, z * 16 + yp * 2).start()
        zp = lax.rem(z + j, 8)
        remote(bloc.at[1], bmid.at[z * 2 + c], ba_s, ba_r, zp * 16 + y * 2 + 1).start()

    @pl.when(c == 0)
    def _():
        remote(bloc.at[1], bmid.at[z * 2], ba_s, ba_r, sib).start()

    @pl.when(c == 1)
    def _():
        remote(bloc.at[0], bmid.at[k], ba_s, ba_r, sib).start()

    bmid[line] = bloc[c]
    xmid[c, slot] = xgo[line]

    by_h = selector(
        lambda o: lax.rem(o, 32) // 2 * 16 + lax.rem(o, 2) * 8 + o // 128 * 4
        + lax.rem(o, 128) // 32,
        256,
    )
    by_p = selector(
        lambda o: o // 128 * 128 + lax.rem(o, 16) // 2 * 16 + lax.rem(o, 128) // 16 * 2
        + lax.rem(o, 2),
        256,
    )

    def arrival(residue):
        zz, yy = residue // 32, lax.rem(residue, 32) // 4
        return lax.rem(residue, 2) + jnp.where(
            lax.rem(residue, 4) // 2 == 0, zz * 16 + yy * 2, 128 + yy * 16 + zz * 2
        )

    natural = selector(arrival, 256)
    by_line = selector(
        lambda o: arrival(device(o // 32, lax.rem(o, 32) // 2) * 2 + lax.rem(o, 2)), 256
    )

    def spread(js):
        for j in js:
            remote(
                bsend, bias.at[j], bb_s.at[j], bb_r.at[j], device(lax.rem(place + j, 8), line)
            ).start()

    got = xgo.at[pl.ds(0, 15)]
    remote(got, got, xa_s, xa_r, sib).wait_recv()
    xsend[...] = pick(by_p, xmid[...].reshape(256, 256)).reshape(2, 8, 16, 256)
    for j in FAR_Z:
        zp, yp = lax.rem(z + j, 8), lax.rem(y + j, 8)
        remote(xsend.at[0, zp], xrows.at[c, 0, z], xb_s, xb_r, zp * 16 + k).start()
        remote(xsend.at[1, yp], xrows.at[c, 1, y], xb_s, xb_r, z * 16 + yp * 2 + c).start()
    xrows[c, 0, z] = xsend[0, z]
    xrows[c, 1, y] = xsend[1, y]

    remote(bmid.at[pl.ds(0, 15)], bmid.at[pl.ds(0, 15)], ba_s, ba_r, sib).wait_recv()
    sorted_bias = pick(by_h, bmid[...].reshape(256, 128))
    bsend[...] = jnp.concatenate([sorted_bias[0:128], sorted_bias[128:256]], axis=1)
    spread(FAR_Z)


    for load in loads[4:]:
        load.wait()
    seq = lax.broadcasted_iota(jnp.int32, (2, 128), 1)
    half = lax.broadcasted_iota(jnp.int32, (1, 256), 1) // 128
    masks = []
    for q in range(2):
        gaps = jnp.sum(jnp.where(seq == me - c + q, flags[...], 0), axis=1, keepdims=True)
        masks.append(jnp.where(half == 0, gaps[0:1], gaps[1:2]) == 1)

    got = xgo.at[pl.ds(0, 14)]
    remote(got, got, xb_s, xb_r, sib).wait_recv()
    swap = remote(xrows.at[c], xrows.at[c], xd_s, xd_r, sib)
    swap.start()
    swap.wait_recv()
    keys = []
    values = []
    for q in range(2):
        normed = normalize(xrows[q].reshape(256, 256).astype(F32), rgain[...])
        ordered = pick(natural, normed)
        keys.append(mm(ordered, rin[1]).astype(BF))
        values.append(
            jnp.concatenate([mm(ordered, rin[2]).astype(BF), jnp.ones((256, 128), BF)], axis=1)
        )
        ordered = pick(by_line, normed)
        query[q] = (mm(ordered, rin[0]) * DEPTH ** (-0.5)).astype(BF)
        gate[q] = jax.nn.sigmoid(mm(ordered, rin[3]))

    lanes = pl.ds(pl.multiple_of(c * 128, 128), 128)
    pair_rows = pl.ds(pl.multiple_of(me - c, 2), 2)
    mine = [head_lanes(h, 32) for h in range(4)]
    keep = pltpu.make_async_copy(
        gsend.at[place, :, line], cols.at[pair_rows, :, lanes], own_sem
    )
    for j in (0,) + FAR_Z:
        p = lax.rem(place + 8 - j, 8)
        block = pl.ds(pl.multiple_of(p * 32, 32), 32)
        if j == 0:
            added = bsend[...].reshape(128, 256).astype(F32)
        else:
            remote(bsend, bsend, bb_s.at[j], bb_r.at[j], sib).wait_recv()
            added = bias[j].reshape(128, 256).astype(F32)
        for q in range(2):
            rows = query[q, block, :]
            stack = jnp.concatenate([jnp.where(m, rows, 0) for m in mine], axis=0)
            scores = mm_nt(stack, keys[q]) + added
            scores = jnp.where(masks[q], MASKED_SCORE, scores)
            scores = scores - jnp.max(scores, axis=1, keepdims=True)
            sums = mm(jnp.exp(scores).astype(BF), values[q])
            top = sum(jnp.where(mine[h], sums[32 * h : 32 * h + 32, 0:128], 0.0) for h in range(4))
            count = sum(
                jnp.where(mine[h], sums[32 * h : 32 * h + 32, 128:256], 0.0) for h in range(4)
            )
            gsend[p, q] = (top / count * gate[q, block, :]).astype(BF).reshape(16, 2, 128)
        for m in (8, 7, 9, 6, 10, 5, 11, 4, 12, 3, 13, 2, 14, 1, 15, 0):
            if j == 0 and m == 0:
                keep.start()
                continue
            n = lax.rem(line + m, 16)
            remote(
                gsend.at[p, :, n], cols.at[pair_rows, :, lanes], g_s, g_r, device(p, n)
            ).start()

    apart = selector(lambda o: lax.rem(o, 128) * 2 + o // 128, 256)
    masked = jnp.where(z // 4 == 0, flags[0:1, :], flags[1:2, :]) == 1
    residual = mm(apart, xloc[...].reshape(256, 256))
    keep.wait()
    got = cols.at[pl.ds(0, 127)]
    remote(got, got, g_s, g_r, sib).wait_recv()

    gated = pick(apart, cols[...].reshape(256, 256))
    first = (residual + mm(gated, rout[...])).astype(BF).astype(F32)
    normed = normalize(first, cgain[...])
    queries = (mm(normed, cin[:, 0:256]) * DEPTH ** (-0.5)).astype(BF)
    keys = mm(normed, cin[:, 256:512]).astype(BF)
    values = mm(normed, cin[:, 512:768]).astype(BF)
    gates = jax.nn.sigmoid(mm(normed, cin[:, 768:1024]))
    attended = []
    for r in range(2):
        q, t, v = (a[128 * r : 128 * r + 128] for a in (queries, keys, values))
        exps = []
        weights = []
        for h in range(HEADS):
            these = head_lanes(h, 128, 256)
            scores = mm_nt(jnp.where(these, q, 0), t)
            scores = jnp.where(masked, MASKED_SCORE, scores)
            scores = scores - jnp.max(scores, axis=1, keepdims=True)
            exps.append(jnp.exp(scores).astype(BF))
            weights.append(value_and_count(these, v))
        total = mm(jnp.concatenate(exps, axis=1), jnp.concatenate(weights, axis=0))
        attended.append(total[:, 0:256] / total[:, 256:512])
    gated = (jnp.concatenate(attended, axis=0) * gates).astype(BF)
    second = (first + mm(gated, cout[...])).astype(BF).astype(F32)
    hidden = jnp.maximum(mm(normalize(second, tgain[...]), wide[...]), 0.0).astype(BF)
    together = selector(lambda o: lax.rem(o, 2) * 128 + o // 2, 256)
    out_ref[...] = pick(together, (second + mm(hidden, shrink[...])).astype(BF))

    remote(bmid.at[pl.ds(0, 15)], bmid.at[pl.ds(0, 15)], ba_s, ba_r, sib).wait_send()
    got = xgo.at[pl.ds(0, 15)]
    remote(got, got, xa_s, xa_r, sib).wait_send()
    got = xgo.at[pl.ds(0, 14)]
    remote(got, got, xb_s, xb_r, sib).wait_send()
    swap.wait_send()
    for j in FAR_Z:
        remote(bsend, bsend, bb_s.at[j], bb_r.at[j], sib).wait_send()
    got = cols.at[pl.ds(0, 127)]
    remote(got, got, g_s, g_r, sib).wait_send()


def finish(rows_ref, out_ref):
    together = selector(lambda o: lax.rem(o, 2) * 128 + o // 2, 256)
    out_ref[...] = pick(together, rows_ref[...]).reshape(128, 2, 256)


def body(
    aligned_chain_features,
    pair_representation_state,
    gap_block_flags,
    pair_norm_gain,
    pair_head_weight,
    horizontal_scaling_factor,
    row_input_weight,
    horizontal_final_matrix,
    vertical_scaling_factor,
    column_input_weight,
    vertical_final_matrix,
    feedforward_scaling_factor,
    feedforward_widen_matrix,
    feedforward_shrink_matrix,
):
    dma = pltpu.SemaphoreType.DMA
    vmem = pl.BlockSpec(memory_space=pltpu.VMEM)
    operands = (
        aligned_chain_features,
        pair_representation_state.reshape(512, 128),
        jnp.transpose(gap_block_flags),
        pair_norm_gain.reshape(1, 128),
        jnp.transpose(pair_head_weight),
        horizontal_scaling_factor.reshape(1, 256),
        row_input_weight,
        horizontal_final_matrix,
        vertical_scaling_factor.reshape(1, 256),
        column_input_weight,
        vertical_final_matrix,
        feedforward_scaling_factor.reshape(1, 256),
        feedforward_widen_matrix,
        feedforward_shrink_matrix,
    )
    copies = [a.shape for a in operands]
    copies[6] = (4, 256, 128)
    rows = pl.pallas_call(
        kernel,
        out_shape=pltpu.VMEM((256, 256), BF),
        in_specs=[pl.BlockSpec(memory_space=pl.ANY)] * len(operands),
        out_specs=vmem,
        scratch_shapes=[pltpu.VMEM(n, a.dtype) for n, a in zip(copies, operands)]
        + [
            pltpu.VMEM((2, 16, 128), BF),
            pltpu.VMEM((16, 16, 128), BF),
            pltpu.VMEM((128, 256), BF),
            pltpu.VMEM((8, 128, 256), BF),
            pltpu.VMEM((16, 16, 256), BF),
            pltpu.VMEM((2, 8, 16, 256), BF),
            pltpu.VMEM((2, 8, 16, 256), BF),
            pltpu.VMEM((2, 2, 8, 16, 256), BF),
            pltpu.VMEM((2, 256, 128), BF),
            pltpu.VMEM((2, 256, 128), F32),
            pltpu.VMEM((8, 2, 16, 2, 128), BF),
            pltpu.VMEM((128, 2, 256), BF),
            dma((13,)), dma((4,)), dma, dma, dma, dma((8,)), dma((8,)),
            dma, dma, dma, dma, dma, dma, dma, dma,
        ],
        name="evoformer",
        compiler_params=pltpu.CompilerParams(
            collective_id=0, has_side_effects=True, vmem_limit_bytes=56 << 20
        ),
    )(*operands)
    return rows.reshape(128, 2, 256)


def solution(mesh):
    placed = (
        P("dp", "res", None),
        P(("dp", "res"), None, None),
        P("dp", None),
        P(),
        P(),
        P(),
        P(),
        P(),
        P(),
        P(),
        P(),
        P(),
        P(),
        P(),
    )
    return jax.shard_map(
        body, mesh=mesh, in_specs=placed, out_specs=P("dp", "res", None), check_vma=False
    )
```

time: 43.7 us -> 41.2 us (0.943)
  Pallas kernels: 41.9 us -> 40.3 us
  local copies, waits for them, and re-layouts: 1.62 us -> 0.71 us
    pallas_call x1, Pallas kernels: 41.9 us -> 40.3 us  [body(): pl.pallas_call(kernel, out_shape=pltpu.VMEM((256, 256), BF), in_specs=[pl...]
    reshape x1, local copies, waits for them, and re-layouts: 1.62 us -> 0.71 us  [body(): return rows.reshape(128, 2, 256)]
where the time goes in v4:
time: 41.2 us; the launch traced here: 41.1 us
  Pallas kernels  40.3 us (98%)
  local copies, waits for them, and re-layouts  0.71 us (2%)
    pallas_call x1, Pallas kernels, body(): pl.pallas_call(kernel, out_shape=pltpu.VMEM((256, 256), BF), in_specs=[pl...  40.3 us

profile of v4, /device:TPU:1, one launch (start us, length us, event | category | flops | bytes accessed | tf_op | source)
XLA Modules:
  0.0 41.1 jit_solution(17284400449578065024)
XLA Ops:
  0.0 40.3 %evoformer.1 = bf16[256,256]{1,0:T(8,128)(2,1)S(1)} custom-call(bf16[128,2,256]{2,1,0:T(2,128)(2,1)} %x_hbm.1, bf16[512,128]{1,0:T(8,128)(2,1)} %bitcast.7, s32[2,128]{1,0:T(2,128)} %bitcast.9, f32[1,128]{1,0:T(1,128)} %bitcast.13, bf16[8,128]{1,0:T(8,128)(2,1)} %bitcast.8, f32[1,256]{1,0:T(1,128)} %bitcast.10, bf16[256,1024]{1,0:T(8,128)(2,1)} %rin_hbm.1, ...), custom_call_target="tpu_custom_call" | custom-call | tf_op jit(solution)/shard_map/evoformer/pallas_call | solution.py:349
  40.3 0.7 %reshape.23 = bf16[128,2,256]{2,1,0:T(2,128)(2,1)} reshape(bf16[256,256]{1,0:T(8,128)(2,1)S(1)} %evoformer.1) | data formatting | bytes 262144 | tf_op jit(solution)/shard_map/reshape | solution.py:376

commit v5 on v4

--- a/solution.py
+++ b/solution.py
@@ -99,8 +99,8 @@
     loads = [
         pltpu.make_async_copy(source, target, load_sem.at[n])
         for n, (source, target) in enumerate((
-            (pair_hbm, pair), (pgain_hbm, pgain), (pw_hbm, pw), (x_hbm, xloc),
-            (flags_hbm, flags), (rgain_hbm, rgain), (rout_hbm, rout),
+            (pair_hbm, pair), (pgain_hbm, pgain), (pw_hbm, pw), (x_hbm, xloc), (rgain_hbm, rgain),
+            (flags_hbm, flags), (rout_hbm, rout),
             (cgain_hbm, cgain), (cin_hbm, cin), (cout_hbm, cout),
             (tgain_hbm, tgain), (wide_hbm, wide), (shrink_hbm, shrink),
         ))
@@ -128,8 +128,10 @@
     by_n = selector(
         lambda o: device(lax.rem(o, 16) // 2, o // 16) * 2 + lax.rem(o, 2), 256
     )
-    loads[3].wait()
-    xgo[...] = pick(by_n, xloc[...].reshape(256, 256)).reshape(16, 16, 256)
+    for load in loads[3:5]:
+        load.wait()
+    normed = normalize(xloc[...].reshape(256, 256).astype(F32), rgain[...])
+    xgo[...] = pick(by_n, normed).reshape(16, 16, 256)
 
     pl.semaphore_wait(barrier, 29)
 
@@ -186,8 +188,8 @@
     xsend[...] = pick(by_p, xmid[...].reshape(256, 256)).reshape(2, 8, 16, 256)
     for j in FAR_Z:
         zp, yp = lax.rem(z + j, 8), lax.rem(y + j, 8)
-        remote(xsend.at[0, zp], xrows.at[c, 0, z], xb_s, xb_r, zp * 16 + k).start()
-        remote(xsend.at[1, yp], xrows.at[c, 1, y], xb_s, xb_r, z * 16 + yp * 2 + c).start()
+        remote(xsend.at[0, zp], xrows.at[c, 0, z], xb_s, xb_r.at[0], zp * 16 + k).start()
+        remote(xsend.at[1, yp], xrows.at[c, 1, y], xb_s, xb_r.at[1], z * 16 + yp * 2 + c).start()
     xrows[c, 0, z] = xsend[0, z]
     xrows[c, 1, y] = xsend[1, y]
 
@@ -197,24 +199,28 @@
     spread(FAR_Z)
 
 
-    for load in loads[4:]:
+    for load in loads[5:]:
         load.wait()
     seq = lax.broadcasted_iota(jnp.int32, (2, 128), 1)
     half = lax.broadcasted_iota(jnp.int32, (1, 256), 1) // 128
     masks = []
-    for q in range(2):
-        gaps = jnp.sum(jnp.where(seq == me - c + q, flags[...], 0), axis=1, keepdims=True)
+    for s in (me, sib):
+        gaps = jnp.sum(jnp.where(seq == s, flags[...], 0), axis=1, keepdims=True)
         masks.append(jnp.where(half == 0, gaps[0:1], gaps[1:2]) == 1)
 
-    got = xgo.at[pl.ds(0, 14)]
-    remote(got, got, xb_s, xb_r, sib).wait_recv()
-    swap = remote(xrows.at[c], xrows.at[c], xd_s, xd_r, sib)
-    swap.start()
-    swap.wait_recv()
+    swaps = []
+    for n in range(2):
+        got = xgo.at[pl.ds(0, 7)]
+        remote(got, got, xb_s, xb_r.at[n], sib).wait_recv()
+        swaps.append(remote(xrows.at[c, n], xrows.at[c, n], xd_s.at[n], xd_r.at[n], sib))
+        swaps[n].start()
     keys = []
     values = []
     for q in range(2):
-        normed = normalize(xrows[q].reshape(256, 256).astype(F32), rgain[...])
+        if q == 1:
+            for swap in swaps:
+                swap.wait_recv()
+        normed = xrows[c if q == 0 else 1 - c].reshape(256, 256)
         ordered = pick(natural, normed)
         keys.append(mm(ordered, rin[1]).astype(BF))
         values.append(
@@ -230,34 +236,41 @@
     keep = pltpu.make_async_copy(
         gsend.at[place, :, line], cols.at[pair_rows, :, lanes], own_sem
     )
-    for j in (0,) + FAR_Z:
-        p = lax.rem(place + 8 - j, 8)
-        block = pl.ds(pl.multiple_of(p * 32, 32), 32)
-        if j == 0:
-            added = bsend[...].reshape(128, 256).astype(F32)
-        else:
-            remote(bsend, bsend, bb_s.at[j], bb_r.at[j], sib).wait_recv()
-            added = bias[j].reshape(128, 256).astype(F32)
+    for pair_of in ((4, 0), (3, 5), (2, 6), (1, 7)):
+        places = [lax.rem(place + 8 - j, 8) for j in pair_of]
+        blocks = [pl.ds(pl.multiple_of(p * 32, 32), 32) for p in places]
+        added = []
+        for j in pair_of:
+            if j == 0:
+                added.append(bsend[...].astype(F32))
+            else:
+                remote(bsend, bsend, bb_s.at[j], bb_r.at[j], sib).wait_recv()
+                added.append(bias[j].astype(F32))
+        added = jnp.concatenate(added, axis=0)
         for q in range(2):
-            rows = query[q, block, :]
-            stack = jnp.concatenate([jnp.where(m, rows, 0) for m in mine], axis=0)
+            stack = jnp.concatenate(
+                [jnp.where(m, query[q, block, :], 0) for block in blocks for m in mine], axis=0
+            )
             scores = mm_nt(stack, keys[q]) + added
             scores = jnp.where(masks[q], MASKED_SCORE, scores)
             scores = scores - jnp.max(scores, axis=1, keepdims=True)
             sums = mm(jnp.exp(scores).astype(BF), values[q])
-            top = sum(jnp.where(mine[h], sums[32 * h : 32 * h + 32, 0:128], 0.0) for h in range(4))
-            count = sum(
-                jnp.where(mine[h], sums[32 * h : 32 * h + 32, 128:256], 0.0) for h in range(4)
-            )
-            gsend[p, q] = (top / count * gate[q, block, :]).astype(BF).reshape(16, 2, 128)
-        for m in (8, 7, 9, 6, 10, 5, 11, 4, 12, 3, 13, 2, 14, 1, 15, 0):
-            if j == 0 and m == 0:
-                keep.start()
-                continue
-            n = lax.rem(line + m, 16)
-            remote(
-                gsend.at[p, :, n], cols.at[pair_rows, :, lanes], g_s, g_r, device(p, n)
-            ).start()
+            for n, (p, block) in enumerate(zip(places, blocks)):
+                parts = [sums[128 * n + 32 * h : 128 * n + 32 * h + 32] for h in range(4)]
+                top = sum(jnp.where(m, part[:, 0:128], 0.0) for m, part in zip(mine, parts))
+                count = sum(jnp.where(m, part[:, 128:256], 0.0) for m, part in zip(mine, parts))
+                gsend[p, c if q == 0 else 1 - c] = (
+                    (top / count * gate[q, block, :]).astype(BF).reshape(16, 2, 128)
+                )
+        for j, p in zip(pair_of, places):
+            for m in (8, 7, 9, 6, 10, 5, 11, 4, 12, 3, 13, 2, 14, 1, 15, 0):
+                if j == 0 and m == 0:
+                    keep.start()
+                    continue
+                n = lax.rem(line + m, 16)
+                remote(
+                    gsend.at[p, :, n], cols.at[pair_rows, :, lanes], g_s, g_r, device(p, n)
+                ).start()
 
     apart = selector(lambda o: lax.rem(o, 128) * 2 + o // 128, 256)
     masked = jnp.where(z // 4 == 0, flags[0:1, :], flags[1:2, :]) == 1
@@ -297,8 +310,9 @@
     got = xgo.at[pl.ds(0, 15)]
     remote(got, got, xa_s, xa_r, sib).wait_send()
     got = xgo.at[pl.ds(0, 14)]
-    remote(got, got, xb_s, xb_r, sib).wait_send()
-    swap.wait_send()
+    remote(got, got, xb_s, xb_r.at[0], sib).wait_send()
+    for swap in swaps:
+        swap.wait_send()
     for j in FAR_Z:
         remote(bsend, bsend, bb_s.at[j], bb_r.at[j], sib).wait_send()
     got = cols.at[pl.ds(0, 127)]
@@ -366,7 +380,7 @@
             pltpu.VMEM((8, 2, 16, 2, 128), BF),
             pltpu.VMEM((128, 2, 256), BF),
             dma((13,)), dma((4,)), dma, dma, dma, dma((8,)), dma((8,)),
-            dma, dma, dma, dma, dma, dma, dma, dma,
+            dma, dma, dma, dma((2,)), dma((2,)), dma((2,)), dma, dma,
         ],
         name="evoformer",
         compiler_params=pltpu.CompilerParams(

time: 41.2 us -> 40.1 us (0.973)
  Pallas kernels: 40.3 us -> 39.2 us
    pallas_call x1, Pallas kernels: 40.3 us -> 39.2 us  [body(): pl.pallas_call(kernel, out_shape=pltpu.VMEM((256, 256), BF), in_specs=[pl...]
where the time goes in v5:
time: 40.1 us; the launch traced here: 39.9 us
  Pallas kernels  39.2 us (98%)
  local copies, waits for them, and re-layouts  0.71 us (2%)
    pallas_call x1, Pallas kernels, body(): pl.pallas_call(kernel, out_shape=pltpu.VMEM((256, 256), BF), in_specs=[pl...  39.2 us

profile of v5, /device:TPU:1, one launch (start us, length us, event | category | flops | bytes accessed | tf_op | source)
XLA Modules:
  0.0 39.9 jit_solution(14870045233405986333)
XLA Ops:
  0.0 39.2 %evoformer.1 = bf16[256,256]{1,0:T(8,128)(2,1)S(1)} custom-call(bf16[128,2,256]{2,1,0:T(2,128)(2,1)} %x_hbm.1, bf16[512,128]{1,0:T(8,128)(2,1)} %bitcast.7, s32[2,128]{1,0:T(2,128)} %bitcast.9, f32[1,128]{1,0:T(1,128)} %bitcast.13, bf16[8,128]{1,0:T(8,128)(2,1)} %bitcast.8, f32[1,256]{1,0:T(1,128)} %bitcast.10, bf16[256,1024]{1,0:T(8,128)(2,1)} %rin_hbm.1, ...), custom_call_target="tpu_custom_call" | custom-call | tf_op jit(solution)/shard_map/evoformer/pallas_call | solution.py:363
  39.2 0.7 %reshape.23 = bf16[128,2,256]{2,1,0:T(2,128)(2,1)} reshape(bf16[256,256]{1,0:T(8,128)(2,1)S(1)} %evoformer.1) | data formatting | bytes 262144 | tf_op jit(solution)/shard_map/reshape | solution.py:390

commit v6 on v5

--- a/solution.py
+++ b/solution.py
@@ -116,14 +116,25 @@
     for load in loads:
         load.start()
 
+    def arrival(residue):
+        zz, yy = residue // 32, lax.rem(residue, 32) // 4
+        return lax.rem(residue, 2) + jnp.where(
+            lax.rem(residue, 4) // 2 == 0, zz * 16 + yy * 2, 128 + yy * 16 + zz * 2
+        )
+
+    column = lax.broadcasted_iota(jnp.int32, (256, 256), 1)
+    residue = lax.broadcasted_iota(jnp.int32, (256, 256), 0)
+    arranged = jnp.where(arrival(residue) == column, 1.0, 0.0).astype(F32).astype(BF)
+
     for load in loads[0:3]:
         load.wait()
     normed = normalize(pair[...].astype(F32), pgain[...])
-    biases = mm_nt(pw[...], normed)
+    biases = mm_nt(pw[...], normed).astype(BF)
+    biases = [mm(biases[:, 256 * n : 256 * n + 256], arranged) for n in range(2)]
     for group in range(2):
-        heads = biases[4 * group : 4 * group + 4]
+        heads = [rows[4 * group : 4 * group + 4] for rows in biases]
         bloc[group] = jnp.concatenate(
-            [heads[:, 128 * n : 128 * n + 128] for n in range(4)], axis=0
+            [rows[:, 128 * n : 128 * n + 128] for rows in heads for n in range(2)], axis=0
         ).astype(BF)
     by_n = selector(
         lambda o: device(lax.rem(o, 16) // 2, o // 16) * 2 + lax.rem(o, 2), 256
@@ -165,14 +176,6 @@
         + lax.rem(o, 2),
         256,
     )
-
-    def arrival(residue):
-        zz, yy = residue // 32, lax.rem(residue, 32) // 4
-        return lax.rem(residue, 2) + jnp.where(
-            lax.rem(residue, 4) // 2 == 0, zz * 16 + yy * 2, 128 + yy * 16 + zz * 2
-        )
-
-    natural = selector(arrival, 256)
     by_line = selector(
         lambda o: arrival(device(o // 32, lax.rem(o, 32) // 2) * 2 + lax.rem(o, 2)), 256
     )
@@ -202,7 +205,8 @@
     for load in loads[5:]:
         load.wait()
     seq = lax.broadcasted_iota(jnp.int32, (2, 128), 1)
-    half = lax.broadcasted_iota(jnp.int32, (1, 256), 1) // 128
+    lane = lax.broadcasted_iota(jnp.int32, (1, 256), 1)
+    half = jnp.where(lane < 128, lane // 16, lax.rem(lane, 16) // 2) // 4
     masks = []
     for s in (me, sib):
         gaps = jnp.sum(jnp.where(seq == s, flags[...], 0), axis=1, keepdims=True)
@@ -221,31 +225,26 @@
             for swap in swaps:
                 swap.wait_recv()
         normed = xrows[c if q == 0 else 1 - c].reshape(256, 256)
-        ordered = pick(natural, normed)
-        keys.append(mm(ordered, rin[1]).astype(BF))
+        keys.append(mm(normed, rin[1]).astype(BF))
         values.append(
-            jnp.concatenate([mm(ordered, rin[2]).astype(BF), jnp.ones((256, 128), BF)], axis=1)
+            jnp.concatenate([mm(normed, rin[2]).astype(BF), jnp.ones((256, 128), BF)], axis=1)
         )
         ordered = pick(by_line, normed)
         query[q] = (mm(ordered, rin[0]) * DEPTH ** (-0.5)).astype(BF)
         gate[q] = jax.nn.sigmoid(mm(ordered, rin[3]))
 
-    lanes = pl.ds(pl.multiple_of(c * 128, 128), 128)
-    pair_rows = pl.ds(pl.multiple_of(me - c, 2), 2)
     mine = [head_lanes(h, 32) for h in range(4)]
     keep = pltpu.make_async_copy(
-        gsend.at[place, :, line], cols.at[pair_rows, :, lanes], own_sem
+        gsend.at[place, line], cols.at[c, me // 2], own_sem
     )
     for pair_of in ((4, 0), (3, 5), (2, 6), (1, 7)):
         places = [lax.rem(place + 8 - j, 8) for j in pair_of]
         blocks = [pl.ds(pl.multiple_of(p * 32, 32), 32) for p in places]
         added = []
         for j in pair_of:
-            if j == 0:
-                added.append(bsend[...].astype(F32))
-            else:
+            if j > 0:
                 remote(bsend, bsend, bb_s.at[j], bb_r.at[j], sib).wait_recv()
-                added.append(bias[j].astype(F32))
+            added.append((bias[j] if j > 0 else bsend[...]).astype(F32))
         added = jnp.concatenate(added, axis=0)
         for q in range(2):
             stack = jnp.concatenate(
@@ -259,7 +258,7 @@
                 parts = [sums[128 * n + 32 * h : 128 * n + 32 * h + 32] for h in range(4)]
                 top = sum(jnp.where(m, part[:, 0:128], 0.0) for m, part in zip(mine, parts))
                 count = sum(jnp.where(m, part[:, 128:256], 0.0) for m, part in zip(mine, parts))
-                gsend[p, c if q == 0 else 1 - c] = (
+                gsend[p, :, c if q == 0 else 1 - c] = (
                     (top / count * gate[q, block, :]).astype(BF).reshape(16, 2, 128)
                 )
         for j, p in zip(pair_of, places):
@@ -269,17 +268,18 @@
                     continue
                 n = lax.rem(line + m, 16)
                 remote(
-                    gsend.at[p, :, n], cols.at[pair_rows, :, lanes], g_s, g_r, device(p, n)
+                    gsend.at[p, n], cols.at[c, me // 2], g_s, g_r, device(p, n)
                 ).start()
 
     apart = selector(lambda o: lax.rem(o, 128) * 2 + o // 128, 256)
     masked = jnp.where(z // 4 == 0, flags[0:1, :], flags[1:2, :]) == 1
     residual = mm(apart, xloc[...].reshape(256, 256))
     keep.wait()
-    got = cols.at[pl.ds(0, 127)]
+    got = xloc.at[pl.ds(0, 127)]
     remote(got, got, g_s, g_r, sib).wait_recv()
 
-    gated = pick(apart, cols[...].reshape(256, 256))
+    halves = [cols[group].reshape(256, 128) for group in range(2)]
+    gated = pick(apart, jnp.concatenate(halves, axis=1))
     first = (residual + mm(gated, rout[...])).astype(BF).astype(F32)
     normed = normalize(first, cgain[...])
     queries = (mm(normed, cin[:, 0:256]) * DEPTH ** (-0.5)).astype(BF)
@@ -303,8 +303,7 @@
     gated = (jnp.concatenate(attended, axis=0) * gates).astype(BF)
     second = (first + mm(gated, cout[...])).astype(BF).astype(F32)
     hidden = jnp.maximum(mm(normalize(second, tgain[...]), wide[...]), 0.0).astype(BF)
-    together = selector(lambda o: lax.rem(o, 2) * 128 + o // 2, 256)
-    out_ref[...] = pick(together, (second + mm(hidden, shrink[...])).astype(BF))
+    out_ref[...] = (second + mm(hidden, shrink[...])).astype(BF)
 
     remote(bmid.at[pl.ds(0, 15)], bmid.at[pl.ds(0, 15)], ba_s, ba_r, sib).wait_send()
     got = xgo.at[pl.ds(0, 15)]
@@ -315,7 +314,7 @@
         swap.wait_send()
     for j in FAR_Z:
         remote(bsend, bsend, bb_s.at[j], bb_r.at[j], sib).wait_send()
-    got = cols.at[pl.ds(0, 127)]
+    got = xloc.at[pl.ds(0, 127)]
     remote(got, got, g_s, g_r, sib).wait_send()
 
 
@@ -377,8 +376,8 @@
             pltpu.VMEM((2, 2, 8, 16, 256), BF),
             pltpu.VMEM((2, 256, 128), BF),
             pltpu.VMEM((2, 256, 128), F32),
-            pltpu.VMEM((8, 2, 16, 2, 128), BF),
-            pltpu.VMEM((128, 2, 256), BF),
+            pltpu.VMEM((8, 16, 2, 2, 128), BF),
+            pltpu.VMEM((2, 64, 2, 2, 128), BF),
             dma((13,)), dma((4,)), dma, dma, dma, dma((8,)), dma((8,)),
             dma, dma, dma, dma((2,)), dma((2,)), dma((2,)), dma, dma,
         ],
@@ -387,7 +386,7 @@
             collective_id=0, has_side_effects=True, vmem_limit_bytes=56 << 20
         ),
     )(*operands)
-    return rows.reshape(128, 2, 256)
+    return jnp.transpose(rows.reshape(2, 128, 256), (1, 0, 2))
 
 
 def solution(mesh):

time: 40.1 us -> 39.8 us (level)
  no operation moved by 1% of the time
where the time goes in v6:
time: 39.8 us; the launch traced here: 39.7 us
  Pallas kernels  38.9 us (98%)
  local copies, waits for them, and re-layouts  0.79 us (2%)
    pallas_call x1, Pallas kernels, body(): pl.pallas_call(kernel, out_shape=pltpu.VMEM((256, 256), BF), in_specs=[pl...  38.9 us

profile of v6, /device:TPU:1, one launch (start us, length us, event | category | flops | bytes accessed | tf_op | source)
XLA Modules:
  0.0 39.7 jit_solution(8156508108192063015)
XLA Ops:
  0.0 38.9 %evoformer.1 = bf16[256,256]{1,0:T(8,128)(2,1)S(1)} custom-call(bf16[128,2,256]{2,1,0:T(2,128)(2,1)} %x_hbm.1, bf16[512,128]{1,0:T(8,128)(2,1)} %bitcast.12, s32[2,128]{1,0:T(2,128)} %bitcast.14, f32[1,128]{1,0:T(1,128)} %bitcast.18, bf16[8,128]{1,0:T(8,128)(2,1)} %bitcast.13, f32[1,256]{1,0:T(1,128)} %bitcast.15, bf16[256,1024]{1,0:T(8,128)(2,1)} %rin_hbm.1, ...), custom_call_target="tpu_custom_call" | custom-call | tf_op jit(solution)/shard_map/evoformer/pallas_call | solution.py:362
  38.9 0.8 %copy.17 = bf16[2,128,256]{2,0,1:T(2,128)(2,1)} copy(bf16[2,128,256]{2,1,0:T(8,128)(2,1)S(1)} %bitcast.11) | data formatting | bytes 262144 | tf_op jit(solution)/shard_map/reshape | solution.py:389

commit v7 on v6

--- a/solution.py
+++ b/solution.py
@@ -113,7 +113,7 @@
         )
         for t in range(4)
     ]
-    for load in loads:
+    for load in loads[:5]:
         load.start()
 
     def arrival(residue):
@@ -163,6 +163,8 @@
     def _():
         remote(bloc.at[0], bmid.at[k], ba_s, ba_r, sib).start()
 
+    for load in loads[5:]:
+        load.start()
     bmid[line] = bloc[c]
     xmid[c, slot] = xgo[line]
 

time: 39.8 us -> 39.9 us (level)
  no operation moved by 1% of the time
where the time goes in v7:
time: 39.9 us; the launch traced here: 39.8 us
  Pallas kernels  39 us (98%)
  local copies, waits for them, and re-layouts  0.79 us (2%)
    pallas_call x1, Pallas kernels, body(): pl.pallas_call(kernel, out_shape=pltpu.VMEM((256, 256), BF), in_specs=[pl...  39 us

profile of v7, /device:TPU:1, one launch (start us, length us, event | category | flops | bytes accessed | tf_op | source)
XLA Modules:
  0.0 39.8 jit_solution(18261866892043134947)
XLA Ops:
  0.0 39.0 %evoformer.1 = bf16[256,256]{1,0:T(8,128)(2,1)S(1)} custom-call(bf16[128,2,256]{2,1,0:T(2,128)(2,1)} %x_hbm.1, bf16[512,128]{1,0:T(8,128)(2,1)} %bitcast.12, s32[2,128]{1,0:T(2,128)} %bitcast.14, f32[1,128]{1,0:T(1,128)} %bitcast.18, bf16[8,128]{1,0:T(8,128)(2,1)} %bitcast.13, f32[1,256]{1,0:T(1,128)} %bitcast.15, bf16[256,1024]{1,0:T(8,128)(2,1)} %rin_hbm.1, ...), custom_call_target="tpu_custom_call" | custom-call | tf_op jit(solution)/shard_map/evoformer/pallas_call | solution.py:364
  39.0 0.8 %copy.17 = bf16[2,128,256]{2,0,1:T(2,128)(2,1)} copy(bf16[2,128,256]{2,1,0:T(8,128)(2,1)S(1)} %bitcast.11) | data formatting | bytes 262144 | tf_op jit(solution)/shard_map/reshape | solution.py:391
